TPU v7x, 32 devices: a whole 2x2x4 slice. The times are simulated.
32 devices in a mesh: dom: 8 (over z, y), lvl: 4 (over x, core).
Axes of the slice: x: 2, y: 2, z: 4, core: 2. Of those that a mesh axis runs over, the one named last changes fastest.
Arguments:
- displacement: float32 [3, 131072], P(None, ('dom', 'lvl')), may hold values from -1.8 to 1.8
- velocity: float32 [3, 131072], P(None, ('dom', 'lvl')), may hold values from -6 to 6
- inverse_mass: float32 [131072], P(('dom', 'lvl')), may hold values from 0.5 to 2
- levels: int32 [2048], P(('dom', 'lvl')), may hold values from 0 to 3, as said below
- first_lame: float32 [2048], P(('dom', 'lvl')), may hold values from 0.125 to 32
- shear_modulus: float32 [2048], P(('dom', 'lvl')), may hold values from 0.125 to 32
- connectivity: int32 [125, 2048], P(None, ('dom', 'lvl')), may hold values from 0 to 4607, as said below
- owner_list: int32 [16384], P(('dom', 'lvl')), may hold values from 0 to 4095, as said below
Outputs:
- new_displacement: float32 [3, 131072], P(None, ('dom', 'lvl'))
- new_velocity: float32 [3, 131072], P(None, ('dom', 'lvl'))
Inputs may be any that keep to these rules, and one draw needn't show every extreme that they name: `levels`: levels 0 to 3. On each device at most 16 elements have level 3, at most 24 level 2 or more, at most 32 level 1 or more; each of these bounds is met on one device of every row of 4 consecutive devices that share a dom index, and every such row holds exactly 32 elements of level 3. `connectivity`: the 125 entries of an element are distinct and form a conforming hexahedral mesh of slabs 2 elements thick chained from device to device in a loop; entries at least 4096 are ghost slots of the next device. `owner_list`: on each device, distinct owned nodes, matching the ghost slots of the previous device.
All inputs are finite; a program needn't handle non-finite values.
Results may differ from a plain program's by a relative error of at most 0.0001.
Values sent between devices are 32-bit elements; how exact they have to be, the bound alone decides.
A program may use at most 64 MiB of HBM per device.

v0:
```python
import functools

import jax
import jax.numpy as jnp
import numpy as np
from jax import lax
from jax.experimental import pallas as pl
from jax.experimental.pallas import tpu as pltpu
from jax.sharding import PartitionSpec as P

substep_length = 0.01
substeps = 8
MESH = pl.DeviceIdType.MESH
f32 = jnp.float32
bf16 = jnp.bfloat16

BLOCK = (
    [(0, 0), (0, 1), (0, 2), (0, 3), (1, 0), (2, 0), (3, 0)]
    + [(b, c) for b in (1, 2, 3) for c in (1, 2, 3)]
)
CENTRE = BLOCK.index((2, 2))
HIGH = [(4, 0), (4, 1), (4, 2), (4, 3), (1, 4), (2, 4), (3, 4), (0, 4)]
PLANES = [(c, a) for c in range(3) for a in range(5)]
MAIN, FACE, TOTAL = 240, 120, 384


def lobatto_tables():
    points = np.array([-1.0, -np.sqrt(3.0 / 7.0), 0.0, np.sqrt(3.0 / 7.0), 1.0])
    weights = np.array([0.1, 49.0 / 90.0, 32.0 / 45.0, 49.0 / 90.0, 0.1])
    factor = np.array(
        [np.prod([points[i] - points[k] for k in range(5) if k != i]) for i in range(5)]
    )
    matrix = np.zeros((5, 5))
    for i in range(5):
        for j in range(5):
            if i == j:
                matrix[i, j] = sum((1.0 / (points[i] - points[k]) for k in range(5) if k != i))
            else:
                matrix[i, j] = factor[i] / (factor[j] * (points[i] - points[j]))
    cube = weights[:, None, None] * weights[None, :, None] * weights[None, None, :]
    return matrix, cube


def element_operator():
    derivative, cube = lobatto_tables()
    one = np.eye(5)
    along = [
        np.kron(np.kron(derivative, one), one),
        np.kron(np.kron(one, derivative), one),
        np.kron(np.kron(one, one), derivative),
    ]
    weight = cube.reshape(125)
    lame = np.zeros((3, 125, 3, 125))
    shear = np.zeros((3, 125, 3, 125))
    for c in range(3):
        for a in range(3):
            lame[c, :, a, :] += along[c].T @ (weight[:, None] * along[a])
            shear[c, :, c, :] += along[a].T @ (weight[:, None] * along[a])
            shear[c, :, a, :] += along[a].T @ (weight[:, None] * along[c])
    rows = []
    for c, a in PLANES:
        rows += [c * 125 + a * 25 + b * 5 + k for b, k in BLOCK]
    for c, a in PLANES:
        rows += [c * 125 + a * 25 + b * 5 + k for b, k in HIGH]
    for c, a in PLANES:
        rows.append(c * 125 + a * 25 + 24)
    rows = np.array(rows)
    full = np.zeros((TOTAL, 2 * TOTAL))
    full[: len(rows), : len(rows)] = lame.reshape(375, 375)[np.ix_(rows, rows)]
    full[: len(rows), TOTAL : TOTAL + len(rows)] = shear.reshape(375, 375)[np.ix_(rows, rows)]
    high = full.astype(jnp.bfloat16)
    low = (full - high.astype(np.float64)).astype(jnp.bfloat16)
    return np.concatenate([high, low], axis=0)


def node_row(a, b, c):
    return a * 25 + b * 5 + c


NAMES = [
    node_row(2, 0, 2), node_row(2, 4, 2),
    node_row(2, 2, 0), node_row(2, 2, 4),
    node_row(2, 0, 0), node_row(2, 4, 4),
    node_row(0, 2, 2), node_row(4, 2, 2),
]


def lanes(shape):
    return lax.broadcasted_iota(jnp.int32, shape, len(shape) - 1)


def sublanes(shape):
    return lax.broadcasted_iota(jnp.int32, shape, len(shape) - 2)


def split_two(x):
    high = x.astype(bf16).astype(f32)
    return jnp.where(lanes(x.shape) < 64, high, x - high).astype(bf16)


def split_three(x):
    high = x.astype(bf16).astype(f32)
    rest = x - high
    middle = rest.astype(bf16).astype(f32)
    first = jnp.where(lanes(x.shape) < 64, high, middle).astype(bf16)
    second = jnp.where(lanes(x.shape) < 64, rest - middle, 0.0).astype(bf16)
    return jnp.concatenate([first, second], axis=1)


def moved(parts, matrix):
    return jnp.dot(parts, matrix, preferred_element_type=f32)


def same(column, row):
    return jnp.where(column == row, 1.0, 0.0).astype(bf16)


def kernel(
    disp_ref, vel_ref, mass_ref, level_ref, lame_ref, shear_ref, conn_ref, owner_ref, oper_ref,
    out_u_ref, out_v_ref,
    conn_s, tile_s, pick_s, hot_hi, hot_lo, u_s, v_s, m_s, f_s, x_s, elem_s,
    low_out, low_in, name_out, name_in, send_buf, recv_buf,
    init_send, init_recv, step_send, step_recv,
):
    dom_size, lvl_size = lax.axis_size("dom"), lax.axis_size("lvl")
    count = dom_size * lvl_size
    me = lax.axis_index("dom") * lvl_size + lax.axis_index("lvl")
    after = lax.rem(me + 1, count)
    before = lax.rem(me + count - 1, count)
    after_id = (after // lvl_size, lax.rem(after, lvl_size))
    before_id = (before // lvl_size, lax.rem(before, lvl_size))

    barrier = pltpu.get_barrier_semaphore()
    for other in (after_id, before_id):
        pl.semaphore_signal(barrier, inc=1, device_id=other, device_id_type=MESH)

    conn_s[:, 0:64] = conn_ref[...]
    conn_s[:, 64:128] = conn_ref[...]
    for row, ref in enumerate((level_ref, lame_ref, shear_ref)):
        elem_s[row : row + 1, 0:64] = ref[...].astype(f32)
        elem_s[row : row + 1, 64:128] = ref[...].astype(f32)

    low_half = lanes((1, 128)) < 64
    for a in range(2):
        for j, (b, c) in enumerate(BLOCK):
            r0, r1 = node_row(a, b, c), node_row(a + 2, b, c)
            pick_s[a * 16 + j : a * 16 + j + 1, :] = jnp.where(
                low_half, conn_s[r0 : r0 + 1, :], conn_s[r1 : r1 + 1, :]
            )
    pick = pick_s[...]
    pick_hi, pick_lo = lax.shift_right_logical(pick, 7), lax.bitwise_and(pick, 127)

    def gather_step(t, kept):
        here = pick_hi == t
        cols = pl.ds(pl.multiple_of(t * 128, 128), 128)
        rows = [disp_ref[c : c + 1, cols] for c in range(3)]
        rows += [vel_ref[c : c + 1, cols] for c in range(3)]
        rows.append(mass_ref[pl.ds(t, 1), :])
        new = []
        for row, old in zip(rows, kept):
            got = jnp.take_along_axis(
                jnp.broadcast_to(row, (32, 128)), pick_lo, axis=1, mode="promise_in_bounds"
            )
            new.append(jnp.where(here, got, old))
        return tuple(new)

    got = lax.fori_loop(
        0, 32, gather_step, tuple(jnp.zeros((32, 128), f32) for _ in range(7)), unroll=4
    )
    half = lanes((32, 128)) < 64
    for k, ref in enumerate([u_s] * 3 + [v_s] * 3 + [m_s]):
        turned = pltpu.roll(got[k], 64, axis=1)
        base = (k % 3) * 80 if k < 6 else 0
        ref[base : base + 32, :] = jnp.where(half, got[k], turned)
        ref[base + 32 : base + 64, :] = jnp.where(half, turned, got[k])
    u_s[MAIN : MAIN + 16, :] = jnp.zeros((16, 128), f32)
    f_s[MAIN : MAIN + 16, :] = jnp.zeros((16, 128), f32)

    tile_s[...] = jnp.zeros((128, 128), f32)
    for k, r in enumerate(NAMES):
        tile_s[k : k + 1, :] = conn_s[r : r + 1, :].astype(f32)
    tile_s[8:12, :] = owner_ref[...].astype(f32)
    columns = jnp.transpose(tile_s[...])
    name_row = [tile_s[k : k + 1, :] for k in range(8)]
    name_col = [columns[:, k : k + 1] for k in range(8)]
    slot_low = jnp.full((1, 128), -9999.0, f32)
    for k in range(4):
        hit = columns[:, 8 + k : 9 + k] == name_row[6]
        number = sublanes((128, 128)).astype(f32) + (k * 128 + 9999)
        slot_low = slot_low + jnp.sum(jnp.where(hit, number, 0.0), axis=0, keepdims=True)
    owned = 4096.0
    slot_high = name_row[7] - owned
    for k in range(3):
        low_out[k * 16 : k * 16 + 16, :] = u_s[k * 80 : k * 80 + 16, :]
        low_out[48 + k * 16 : 64 + k * 16, :] = v_s[k * 80 : k * 80 + 16, :]
    low_out[96:112, :] = m_s[0:16, :]
    low_out[112:120, :] = jnp.broadcast_to(slot_low, (8, 128))
    name_out[...] = jnp.broadcast_to(slot_high, (8, 128))

    pl.semaphore_wait(barrier, 2)
    low_copy = pltpu.make_async_remote_copy(
        src_ref=low_out, dst_ref=low_in, send_sem=init_send.at[0], recv_sem=init_recv.at[0],
        device_id=before_id, device_id_type=MESH,
    )
    name_copy = pltpu.make_async_remote_copy(
        src_ref=name_out, dst_ref=name_in, send_sem=init_send.at[1], recv_sem=init_recv.at[1],
        device_id=after_id, device_id_type=MESH,
    )
    low_copy.start()
    name_copy.start()

    spread = jnp.concatenate(
        [same(name_col[0], name_row[1]), same(name_col[2], name_row[3])], axis=1
    )
    spread = jnp.concatenate([spread, spread], axis=0)
    spread_edge = same(name_col[4], name_row[5])
    spread_edge = jnp.concatenate([spread_edge, spread_edge], axis=0)
    collect = jnp.concatenate(
        [same(name_col[1], name_row[0]), same(name_col[3], name_row[2])], axis=1
    )
    collect_edge = same(name_col[5], name_row[4])
    to_high = same(name_col[6], name_row[7])
    to_low = same(name_col[7], name_row[6])

    row_hi, row_lo = pick_hi, pick_lo
    for r in range(32):
        cols = slice(r * 128, r * 128 + 128)
        hit = row_hi[r : r + 1, :] == sublanes((32, 128))
        hot_hi[0:32, cols] = jnp.where(hit, lanes((32, 128)).astype(f32), 0.0).astype(bf16)
        hot_hi[32:64, cols] = jnp.where(hit, float(r), 0.0).astype(bf16)
        hot_lo[:, cols] = same(sublanes((128, 128)), row_lo[r : r + 1, :])
    place = lax.dot_general(
        hot_hi[...], hot_lo[...], (((1,), (1,)), ((), ())), preferred_element_type=f32
    )
    place_lane = place[0:32].astype(jnp.int32)
    place_row = place[32:64].astype(jnp.int32)

    low_copy.wait()
    name_copy.wait()
    tile_s[0:8, :] = low_in[112:120, :]
    tile_s[8:16, :] = name_in[...]
    columns = jnp.transpose(tile_s[...])
    from_after = same(columns[:, 0:1], slot_high)
    from_before = same(columns[:, 8:9], slot_low)
    to_high_twice = jnp.concatenate([to_high, to_high], axis=0)
    from_after_twice = jnp.concatenate([from_after, from_after], axis=0)
    high = moved(split_three(low_out[0:112, :]), to_high_twice)
    high = high + moved(split_three(low_in[0:112, :]), from_after_twice)
    for k in range(3):
        u_s[k * 80 + 64 : k * 80 + 80, :] = high[k * 16 : k * 16 + 16]
        v_s[k * 80 + 64 : k * 80 + 80, :] = high[48 + k * 16 : 64 + k * 16]
    m_s[64:80, :] = high[96:112]

    level = elem_s[0:1, :]
    period = jnp.where(level == 0.0, 8, jnp.where(level == 1.0, 4, jnp.where(level == 2.0, 2, 1)))
    row8 = sublanes((15, 8, 128))

    def advance(rows, force):
        c_rows = pl.ds(rows[0] * 80 + rows[1] * 16, 16)
        mass = m_s[pl.ds(rows[1] * 16, 16), :]
        speed = v_s[c_rows, :] - substep_length * mass * force
        v_s[c_rows, :] = speed
        u_s[c_rows, :] = u_s[c_rows, :] + substep_length * speed

    def substep(s, carry):
        u = u_s[0:MAIN, :].reshape(15, 16, 128)
        faces = moved(split_three(u[:, 0:8].reshape(FACE, 128)), spread)
        along_y = faces[:, 0:128].reshape(15, 8, 128)
        along_z = faces[:, 128:256].reshape(15, 8, 128)
        face = jnp.where(
            row8 < 4, along_y, jnp.where(row8 < 7, along_z, pltpu.roll(along_z, 7, axis=1))
        )
        edge = moved(split_three(u_s[pl.ds(0, 16, stride=16), :]), spread_edge)
        centres = [
            u_s[c * 80 + 32 + CENTRE : c * 80 + 33 + CENTRE, :] for c in range(3)
        ]
        row16 = sublanes((16, 128))
        edge = edge - jnp.where(
            row16 < 5, centres[0], jnp.where(row16 < 10, centres[1], centres[2])
        )
        edge = jnp.where(row16 < 15, edge, 0.0)
        active = lax.rem(jnp.full((1, 128), s, jnp.int32), period) == 0
        weight = jnp.where(active, period.astype(f32), 0.0)
        for part, value in enumerate((elem_s[1:2, :] * weight, elem_s[2:3, :] * weight)):
            at = part * TOTAL
            for c in range(3):
                main = (u[c * 5 : c * 5 + 5].reshape(80, 128) - centres[c]) * value
                x_s[at + c * 80 : at + c * 80 + 80, :] = split_two(main)
            both = [
                (face[c * 5 : c * 5 + 5].reshape(40, 128) - centres[c]) * value for c in range(3)
            ]
            both += [edge * value, jnp.zeros((8, 128), f32)]
            x_s[at + MAIN : at + TOTAL, :] = split_two(jnp.concatenate(both, axis=0))
        product = jnp.dot(oper_ref[...], x_s[...], preferred_element_type=f32)
        force = product[0:TOTAL] + product[TOTAL : 2 * TOTAL]
        force = force + pltpu.roll(force, 64, axis=1)

        face = moved(split_two(force[MAIN : MAIN + FACE]), collect)
        along_y = face[:, 0:128].reshape(15, 8, 128)
        along_z = face[:, 128:256].reshape(15, 8, 128)
        low = jnp.where(row8 < 4, along_y, jnp.where(row8 < 7, along_z, 0.0))
        low = low + jnp.where(row8 == 0, pltpu.roll(along_z, 1, axis=1), 0.0)
        main = force[0:MAIN].reshape(15, 2, 8, 128)
        main = jnp.concatenate([main[:, 0:1] + low[:, None], main[:, 1:2]], axis=1)
        f_s[0:MAIN, :] = main.reshape(MAIN, 128)
        edge = moved(split_two(force[MAIN + FACE : MAIN + FACE + 16]), collect_edge)
        f_s[pl.ds(0, 16, stride=16), :] = f_s[pl.ds(0, 16, stride=16), :] + edge

        low_x = jnp.concatenate([f_s[c * 80 : c * 80 + 16, :] for c in range(3)], axis=0)
        high_x = jnp.concatenate([f_s[c * 80 + 64 : c * 80 + 80, :] for c in range(3)], axis=0)
        send_buf[s, 0] = low_x
        send_buf[s, 1] = high_x
        copies = [
            pltpu.make_async_remote_copy(
                src_ref=send_buf.at[s, way], dst_ref=recv_buf.at[s, way],
                send_sem=step_send.at[s, way], recv_sem=step_recv.at[s, way],
                device_id=other, device_id_type=MESH,
            )
            for way, other in enumerate((before_id, after_id))
        ]
        copies[1].start()
        copies[0].start()
        low_sum = low_x + moved(split_two(high_x), to_low)
        high_sum = high_x + moved(split_two(low_x), to_high)
        for c in range(3):
            for a in (1, 2, 3):
                advance((c, a), f_s[c * 80 + a * 16 : c * 80 + a * 16 + 16, :])
        copies[1].wait()
        copies[0].wait()
        low_sum = low_sum + moved(split_two(recv_buf[s, 1]), from_before)
        high_sum = high_sum + moved(split_two(recv_buf[s, 0]), from_after)
        for c in range(3):
            advance((c, 0), low_sum[c * 16 : c * 16 + 16])
            advance((c, 4), high_sum[c * 16 : c * 16 + 16])
        return carry

    lax.fori_loop(0, substeps, substep, 0)

    for ref in (u_s, v_s):
        for c in range(3):
            first = ref[c * 80 : c * 80 + 32, :]
            second = ref[c * 80 + 32 : c * 80 + 64, :]
            at = (0 if ref is u_s else 96) + c * 32
            f_s[at : at + 32, :] = jnp.where(half, first, second)

    def scatter_step(t, kept):
        here = place_row == t
        new = []
        for k in range(6):
            row = f_s[pl.ds(k * 32 + t, 1), :]
            got = jnp.take_along_axis(
                jnp.broadcast_to(row, (32, 128)), place_lane, axis=1, mode="promise_in_bounds"
            )
            new.append(jnp.where(here, got, kept[k]))
        return tuple(new)

    done = lax.fori_loop(
        0, 32, scatter_step, tuple(jnp.zeros((32, 128), f32) for _ in range(6)), unroll=4
    )
    for k in range(6):
        ref = out_u_ref if k < 3 else out_v_ref
        for t in range(32):
            ref[k % 3 : k % 3 + 1, t * 128 : t * 128 + 128] = done[k][t : t + 1]


def per_device(
    displacement, velocity, inverse_mass, levels, first_lame, shear_modulus, connectivity, owner_list
):
    operator = jnp.asarray(element_operator())
    nodes = displacement.shape[1]
    vmem = pl.BlockSpec(memory_space=pltpu.VMEM)
    shape = jax.ShapeDtypeStruct((3, nodes), f32)
    V, S = pltpu.VMEM, pltpu.SemaphoreType.DMA
    return pl.pallas_call(
        kernel,
        out_shape=(shape, shape),
        in_specs=[vmem] * 9,
        out_specs=(vmem, vmem),
        scratch_shapes=[
            V((125, 128), jnp.int32), V((128, 128), f32), V((32, 128), jnp.int32),
            V((64, 4096), bf16), V((128, 4096), bf16),
            V((256, 128), f32), V((256, 128), f32), V((80, 128), f32), V((256, 128), f32),
            V((2 * TOTAL, 128), bf16), V((8, 128), f32),
            V((120, 128), f32), V((120, 128), f32), V((8, 128), f32), V((8, 128), f32),
            V((substeps, 2, 48, 128), f32), V((substeps, 2, 48, 128), f32),
            S((2,)), S((2,)), S((substeps, 2)), S((substeps, 2)),
        ],
        compiler_params=pltpu.CompilerParams(
            collective_id=0, has_side_effects=True, vmem_limit_bytes=32 * 1024 * 1024
        ),
    )(
        displacement, velocity, inverse_mass.reshape(32, 128),
        levels.reshape(1, 64), first_lame.reshape(1, 64), shear_modulus.reshape(1, 64),
        connectivity, owner_list.reshape(4, 128), operator,
    )


def solution(mesh):
    in_specs = (
        P(None, ("dom", "lvl")),
        P(None, ("dom", "lvl")),
        P(("dom", "lvl")),
        P(("dom", "lvl")),
        P(("dom", "lvl")),
        P(("dom", "lvl")),
        P(None, ("dom", "lvl")),
        P(("dom", "lvl")),
    )
    out_specs = (P(None, ("dom", "lvl")), P(None, ("dom", "lvl")))
    return jax.shard_map(
        per_device, mesh=mesh, in_specs=in_specs, out_specs=out_specs, check_vma=False
    )
```

profile of v0, /device:TPU:0, one launch (start us, length us, event | category | flops | bytes accessed | tf_op | source)
XLA Modules:
  0.0 65.9 jit_solution(8927881231836470236)
XLA Ops:
  0.6 0.9 %copy.11.conn_ref = s32[125,64]{1,0:T(8,128)S(1)} copy(s32[125,64]{0,1:T(8,128)} %param.15) | data formatting | bytes 64000 | tf_op args[6]
  1.5 0.0 copy-start
  1.5 1.3 %copy-done = bf16[768,768]{1,0:T(8,128)(2,1)S(1)} copy-done((bf16[768,768]{1,0:T(8,128)(2,1)S(1)}, bf16[768,768]{1,0:T(8,128)(2,1)}, u32[]{:S(2)}) %copy-start) | copy-done | bytes 1179672
  2.8 0.0 copy-start.1
  2.8 0.8 %copy-done.1 = f32[3,4096]{1,0:T(4,128)S(1)} copy-done((f32[3,4096]{1,0:T(4,128)S(1)}, f32[3,4096]{1,0:T(4,128)}, u32[]{:S(2)}) %copy-start.1) | copy-done | bytes 49176
  3.6 0.0 copy-start.2
  3.6 0.8 %copy-done.2 = f32[3,4096]{1,0:T(4,128)S(1)} copy-done((f32[3,4096]{1,0:T(4,128)S(1)}, f32[3,4096]{1,0:T(4,128)}, u32[]{:S(2)}) %copy-start.2) | copy-done | bytes 49176
  4.5 0.0 copy-start.3
  4.5 0.7 %copy-done.3 = f32[4096]{0:T(1024)S(1)} copy-done((f32[4096]{0:T(1024)S(1)}, f32[4096]{0:T(1024)}, u32[]{:S(2)}) %copy-start.3) | copy-done | bytes 16408
  5.2 0.0 copy-start.4
  5.2 0.7 %copy-done.4 = s32[512]{0:T(512)S(1)} copy-done((s32[512]{0:T(512)S(1)}, s32[512]{0:T(512)}, u32[]{:S(2)}) %copy-start.4) | copy-done | bytes 2072
  5.9 0.0 copy-start.5
  5.9 0.7 copy-done.5
  6.5 0.0 copy-start.6
  6.5 0.7 copy-done.6
  7.2 0.0 copy-start.7
  7.2 0.7 copy-done.7
  7.8 56.9 %shard_map.104 = (f32[3,4096]{1,0:T(4,128)S(1)}, f32[3,4096]{1,0:T(4,128)S(1)}) custom-call(f32[3,4096]{1,0:T(4,128)S(1)} %copy-done.1, f32[3,4096]{1,0:T(4,128)S(1)} %copy-done.2, f32[32,128]{1,0:T(8,128)S(1)} %bitcast.5, s32[1,64]{1,0:T(1,128)S(1)} %bitcast.7, f32[1,64]{1,0:T(1,128)S(1)} %bitcast.8, f32[1,64]{1,0:T(1,128)S(1)} %bitcast.9, ...), custom_call_target="tpu_custom_call" | custom-call | tf_op jit(solution)/shard_map/pallas_call | solution.py:374
  64.7 0.6 copy.14
  65.3 0.6 copy.15
Async XLA Ops:
  1.5 1.3 %copy-start = (bf16[768,768]{1,0:T(8,128)(2,1)S(1)}, bf16[768,768]{1,0:T(8,128)(2,1)}, u32[]{:S(2)}) copy-start(bf16[768,768]{1,0:T(8,128)(2,1)} %constant.2.clone.oper_ref) | copy-start | bytes 3538948
  2.8 0.8 %copy-start.1 = (f32[3,4096]{1,0:T(4,128)S(1)}, f32[3,4096]{1,0:T(4,128)}, u32[]{:S(2)}) copy-start(f32[3,4096]{1,0:T(4,128)} %disp_ref.1) | copy-start | bytes 147460
  3.6 0.8 %copy-start.2 = (f32[3,4096]{1,0:T(4,128)S(1)}, f32[3,4096]{1,0:T(4,128)}, u32[]{:S(2)}) copy-start(f32[3,4096]{1,0:T(4,128)} %vel_ref.1) | copy-start | bytes 147460
  4.5 0.7 %copy-start.3 = (f32[4096]{0:T(1024)S(1)}, f32[4096]{0:T(1024)}, u32[]{:S(2)}) copy-start(f32[4096]{0:T(1024)} %param.11) | copy-start | bytes 49156
  5.2 0.7 %copy-start.4 = (s32[512]{0:T(512)S(1)}, s32[512]{0:T(512)}, u32[]{:S(2)}) copy-start(s32[512]{0:T(512)} %param.16) | copy-start | bytes 6148
  5.9 0.7 copy-start.5
  6.5 0.7 copy-start.6
  7.2 0.7 copy-start.7
where the time goes:
time: 66.4 us; the launch traced here: 65.9 us
  Pallas kernels  56.9 us (86%)
  local copies, waits for them, and re-layouts  8.43 us (13%)
    pallas_call x1, Pallas kernels, per_device(): pl.pallas_call(kernel, out_shape=(shape, shape), in_specs=[vmem] * 9, out...  56.9 us
    unnamed x19, local copies, waits for them, and re-layouts  8.43 us

commit v1 on v0

--- a/solution.py
+++ b/solution.py
@@ -115,30 +115,82 @@
     return jnp.where(column == row, 1.0, 0.0).astype(bf16)
 
 
+FOLDED = [5, 1, 3, 2, 0, 4, 6, 7, 11, 10, 8, 12, 14, 15, 13, 9]
+STATE, NAMED, ROWS = 224, 232, 240
+
+
+def looked_up(index, table):
+    found = jnp.int32(table[0])
+    for k, value in enumerate(table[1:], 1):
+        found = jnp.where(index == k, jnp.int32(value), found)
+    return found
+
+
 def kernel(
-    disp_ref, vel_ref, mass_ref, level_ref, lame_ref, shear_ref, conn_ref, owner_ref, oper_ref,
+    folded, disp_hbm, vel_hbm, mass_hbm, level_hbm, lame_hbm, shear_hbm, conn_hbm, owner_hbm, oper_hbm,
     out_u_ref, out_v_ref,
+    disp_ref, vel_ref, mass_ref, level_ref, lame_ref, shear_ref, conn_ref, owner_ref, oper_ref, load_sem,
     conn_s, tile_s, pick_s, hot_hi, hot_lo, u_s, v_s, m_s, f_s, x_s, elem_s,
+    pack_out, pack_in, back_out, back_in,
     low_out, low_in, name_out, name_in, send_buf, recv_buf,
-    init_send, init_recv, step_send, step_recv,
+    init_send, init_recv, step_send, step_recv, bulk_send, bulk_recv,
 ):
     dom_size, lvl_size = lax.axis_size("dom"), lax.axis_size("lvl")
     count = dom_size * lvl_size
     me = lax.axis_index("dom") * lvl_size + lax.axis_index("lvl")
-    after = lax.rem(me + 1, count)
-    before = lax.rem(me + count - 1, count)
-    after_id = (after // lvl_size, lax.rem(after, lvl_size))
-    before_id = (before // lvl_size, lax.rem(before, lvl_size))
+
+    loads = [
+        pltpu.make_async_copy(src, dst, load_sem.at[k])
+        for k, (src, dst) in enumerate([
+            (conn_hbm, conn_ref), (disp_hbm, disp_ref), (vel_hbm, vel_ref), (mass_hbm, mass_ref),
+            (owner_hbm, owner_ref), (level_hbm, level_ref), (lame_hbm, lame_ref),
+            (shear_hbm, shear_ref), (oper_hbm, oper_ref),
+        ])
+    ]
+    for load in loads:
+        load.start()
+
+    def device(index):
+        return (index // lvl_size, lax.rem(index, lvl_size))
+
+    if folded:
+        chips = count // 2
+        chip, core = me // 2, lax.rem(me, 2)
+        order = [FOLDED.index(k) for k in range(chips)]
+        host = looked_up(chip, FOLDED) * 2 + core
+        home = looked_up(chip, order) * 2 + core
+        after_chip = looked_up(chip, [FOLDED[(k + 1) % chips] for k in order])
+        before_chip = looked_up(chip, [FOLDED[k - 1] for k in order])
+        after = jnp.where(core == 1, after_chip * 2, me + 1)
+        before = jnp.where(core == 1, me - 1, before_chip * 2 + 1)
+        host_id, home_id = device(host), device(home)
+        away = host != me
+    else:
+        after = lax.rem(me + 1, count)
+        before = lax.rem(me + count - 1, count)
+    after_id, before_id = device(after), device(before)
 
     barrier = pltpu.get_barrier_semaphore()
     for other in (after_id, before_id):
         pl.semaphore_signal(barrier, inc=1, device_id=other, device_id_type=MESH)
-
-    conn_s[:, 0:64] = conn_ref[...]
-    conn_s[:, 64:128] = conn_ref[...]
-    for row, ref in enumerate((level_ref, lame_ref, shear_ref)):
-        elem_s[row : row + 1, 0:64] = ref[...].astype(f32)
-        elem_s[row : row + 1, 64:128] = ref[...].astype(f32)
+    if folded:
+
+        @pl.when(away)
+        def _():
+            for other in (host_id, home_id):
+                pl.semaphore_signal(barrier, inc=1, device_id=other, device_id_type=MESH)
+
+    def bulk(src, dst, k, other):
+        return pltpu.make_async_remote_copy(
+            src_ref=src, dst_ref=dst, send_sem=bulk_send.at[k], recv_sem=bulk_recv.at[k],
+            device_id=other, device_id_type=MESH,
+        )
+
+    loads[0].wait()
+    tile_s[...] = jnp.zeros((128, 128), f32)
+    for k in range(2):
+        tile_s[k * 64 : k * 64 + 64, 0:125] = conn_ref[...].astype(f32)
+    conn_s[...] = jnp.transpose(tile_s[...])
 
     low_half = lanes((1, 128)) < 64
     for a in range(2):
@@ -146,9 +198,12 @@
             r0, r1 = node_row(a, b, c), node_row(a + 2, b, c)
             pick_s[a * 16 + j : a * 16 + j + 1, :] = jnp.where(
                 low_half, conn_s[r0 : r0 + 1, :], conn_s[r1 : r1 + 1, :]
-            )
+            ).astype(jnp.int32)
     pick = pick_s[...]
     pick_hi, pick_lo = lax.shift_right_logical(pick, 7), lax.bitwise_and(pick, 127)
+
+    for load in loads[1:8]:
+        load.wait()
 
     def gather_step(t, kept):
         here = pick_hi == t
@@ -168,36 +223,83 @@
         0, 32, gather_step, tuple(jnp.zeros((32, 128), f32) for _ in range(7)), unroll=4
     )
     half = lanes((32, 128)) < 64
+    for k in range(7):
+        pack_out[k * 32 : k * 32 + 32, :] = got[k]
+
+    for k, r in enumerate(NAMES):
+        pack_out[STATE + k : STATE + k + 1, :] = conn_s[r : r + 1, :]
+    tile_s[0:8, :] = jnp.zeros((8, 128), f32)
+    tile_s[0:4, :] = owner_ref[...].astype(f32)
+    columns = jnp.transpose(tile_s[...])
+    low_name = conn_s[NAMES[6] : NAMES[6] + 1, :]
+    slot_low = jnp.full((1, 128), -9999.0, f32)
+    for k in range(4):
+        hit = columns[:, k : k + 1] == low_name
+        number = sublanes((128, 128)).astype(f32) + (k * 128 + 9999)
+        slot_low = slot_low + jnp.sum(jnp.where(hit, number, 0.0), axis=0, keepdims=True)
+    pack_out[NAMED : NAMED + 8, :] = jnp.zeros((8, 128), f32)
+    pack_out[NAMED : NAMED + 1, :] = slot_low
+    for k, ref in enumerate((level_ref, lame_ref, shear_ref), 1):
+        for at in (0, 64):
+            pack_out[NAMED + k : NAMED + k + 1, at : at + 64] = ref[...].astype(f32)
+
+    if folded:
+
+        @pl.when(away)
+        def _():
+            pl.semaphore_wait(barrier, 4)
+            bulk(pack_out, pack_in, 0, host_id).start()
+
+        @pl.when(jnp.logical_not(away))
+        def _():
+            pl.semaphore_wait(barrier, 2)
+    else:
+        pl.semaphore_wait(barrier, 2)
+
+    def find_places():
+        for r in range(32):
+            cols = slice(r * 128, r * 128 + 128)
+            hit = pick_hi[r : r + 1, :] == sublanes((32, 128))
+            hot_hi[0:32, cols] = jnp.where(hit, lanes((32, 128)).astype(f32), 0.0).astype(bf16)
+            hot_hi[32:64, cols] = jnp.where(hit, float(r), 0.0).astype(bf16)
+            hot_lo[:, cols] = same(sublanes((128, 128)), pick_lo[r : r + 1, :])
+        place = lax.dot_general(
+            hot_hi[...], hot_lo[...], (((1,), (1,)), ((), ())), preferred_element_type=f32
+        )
+        return place[0:32].astype(jnp.int32), place[32:64].astype(jnp.int32)
+
+    if folded:
+        place_lane, place_row = find_places()
+
+        @pl.when(away)
+        def _():
+            bulk(pack_out, pack_in, 0, host_id).wait()
+
+        @pl.when(jnp.logical_not(away))
+        def _():
+            pack_in[...] = pack_out[...]
+
+    held = pack_in if folded else pack_out
     for k, ref in enumerate([u_s] * 3 + [v_s] * 3 + [m_s]):
-        turned = pltpu.roll(got[k], 64, axis=1)
+        packed = held[k * 32 : k * 32 + 32, :]
+        turned = pltpu.roll(packed, 64, axis=1)
         base = (k % 3) * 80 if k < 6 else 0
-        ref[base : base + 32, :] = jnp.where(half, got[k], turned)
-        ref[base + 32 : base + 64, :] = jnp.where(half, turned, got[k])
+        ref[base : base + 32, :] = jnp.where(half, packed, turned)
+        ref[base + 32 : base + 64, :] = jnp.where(half, turned, packed)
     u_s[MAIN : MAIN + 16, :] = jnp.zeros((16, 128), f32)
     f_s[MAIN : MAIN + 16, :] = jnp.zeros((16, 128), f32)
-
-    tile_s[...] = jnp.zeros((128, 128), f32)
-    for k, r in enumerate(NAMES):
-        tile_s[k : k + 1, :] = conn_s[r : r + 1, :].astype(f32)
-    tile_s[8:12, :] = owner_ref[...].astype(f32)
-    columns = jnp.transpose(tile_s[...])
-    name_row = [tile_s[k : k + 1, :] for k in range(8)]
-    name_col = [columns[:, k : k + 1] for k in range(8)]
-    slot_low = jnp.full((1, 128), -9999.0, f32)
-    for k in range(4):
-        hit = columns[:, 8 + k : 9 + k] == name_row[6]
-        number = sublanes((128, 128)).astype(f32) + (k * 128 + 9999)
-        slot_low = slot_low + jnp.sum(jnp.where(hit, number, 0.0), axis=0, keepdims=True)
-    owned = 4096.0
+    elem_s[...] = held[NAMED : NAMED + 8, :]
+    slot_low = elem_s[0:1, :]
+    name_row = [held[STATE + k : STATE + k + 1, :] for k in range(8)]
+    owned = float(disp_ref.shape[1])
     slot_high = name_row[7] - owned
+
     for k in range(3):
         low_out[k * 16 : k * 16 + 16, :] = u_s[k * 80 : k * 80 + 16, :]
         low_out[48 + k * 16 : 64 + k * 16, :] = v_s[k * 80 : k * 80 + 16, :]
     low_out[96:112, :] = m_s[0:16, :]
     low_out[112:120, :] = jnp.broadcast_to(slot_low, (8, 128))
     name_out[...] = jnp.broadcast_to(slot_high, (8, 128))
-
-    pl.semaphore_wait(barrier, 2)
     low_copy = pltpu.make_async_remote_copy(
         src_ref=low_out, dst_ref=low_in, send_sem=init_send.at[0], recv_sem=init_recv.at[0],
         device_id=before_id, device_id_type=MESH,
@@ -209,6 +311,9 @@
     low_copy.start()
     name_copy.start()
 
+    tile_s[0:8, :] = held[STATE : STATE + 8, :]
+    columns = jnp.transpose(tile_s[...])
+    name_col = [columns[:, k : k + 1] for k in range(8)]
     spread = jnp.concatenate(
         [same(name_col[0], name_row[1]), same(name_col[2], name_row[3])], axis=1
     )
@@ -221,19 +326,8 @@
     collect_edge = same(name_col[5], name_row[4])
     to_high = same(name_col[6], name_row[7])
     to_low = same(name_col[7], name_row[6])
-
-    row_hi, row_lo = pick_hi, pick_lo
-    for r in range(32):
-        cols = slice(r * 128, r * 128 + 128)
-        hit = row_hi[r : r + 1, :] == sublanes((32, 128))
-        hot_hi[0:32, cols] = jnp.where(hit, lanes((32, 128)).astype(f32), 0.0).astype(bf16)
-        hot_hi[32:64, cols] = jnp.where(hit, float(r), 0.0).astype(bf16)
-        hot_lo[:, cols] = same(sublanes((128, 128)), row_lo[r : r + 1, :])
-    place = lax.dot_general(
-        hot_hi[...], hot_lo[...], (((1,), (1,)), ((), ())), preferred_element_type=f32
-    )
-    place_lane = place[0:32].astype(jnp.int32)
-    place_row = place[32:64].astype(jnp.int32)
+    if not folded:
+        place_lane, place_row = find_places()
 
     low_copy.wait()
     name_copy.wait()
@@ -250,8 +344,9 @@
         u_s[k * 80 + 64 : k * 80 + 80, :] = high[k * 16 : k * 16 + 16]
         v_s[k * 80 + 64 : k * 80 + 80, :] = high[48 + k * 16 : 64 + k * 16]
     m_s[64:80, :] = high[96:112]
-
-    level = elem_s[0:1, :]
+    loads[8].wait()
+
+    level = elem_s[1:2, :]
     period = jnp.where(level == 0.0, 8, jnp.where(level == 1.0, 4, jnp.where(level == 2.0, 2, 1)))
     row8 = sublanes((15, 8, 128))
 
@@ -281,7 +376,7 @@
         edge = jnp.where(row16 < 15, edge, 0.0)
         active = lax.rem(jnp.full((1, 128), s, jnp.int32), period) == 0
         weight = jnp.where(active, period.astype(f32), 0.0)
-        for part, value in enumerate((elem_s[1:2, :] * weight, elem_s[2:3, :] * weight)):
+        for part, value in enumerate((elem_s[2:3, :] * weight, elem_s[3:4, :] * weight)):
             at = part * TOTAL
             for c in range(3):
                 main = (u[c * 5 : c * 5 + 5].reshape(80, 128) - centres[c]) * value
@@ -308,8 +403,9 @@
 
         low_x = jnp.concatenate([f_s[c * 80 : c * 80 + 16, :] for c in range(3)], axis=0)
         high_x = jnp.concatenate([f_s[c * 80 + 64 : c * 80 + 80, :] for c in range(3)], axis=0)
-        send_buf[s, 0] = low_x
-        send_buf[s, 1] = high_x
+        half24 = lanes((24, 128)) < 64
+        send_buf[s, 0] = jnp.where(half24, low_x[0:24], low_x[24:48])
+        send_buf[s, 1] = jnp.where(half24, high_x[0:24], high_x[24:48])
         copies = [
             pltpu.make_async_remote_copy(
                 src_ref=send_buf.at[s, way], dst_ref=recv_buf.at[s, way],
@@ -327,8 +423,15 @@
                 advance((c, a), f_s[c * 80 + a * 16 : c * 80 + a * 16 + 16, :])
         copies[1].wait()
         copies[0].wait()
-        low_sum = low_sum + moved(split_two(recv_buf[s, 1]), from_before)
-        high_sum = high_sum + moved(split_two(recv_buf[s, 0]), from_after)
+
+        def unpacked(packed):
+            turned = pltpu.roll(packed, 64, axis=1)
+            return jnp.concatenate(
+                [jnp.where(half24, packed, turned), jnp.where(half24, turned, packed)], axis=0
+            )
+
+        low_sum = low_sum + moved(split_two(unpacked(recv_buf[s, 1])), from_before)
+        high_sum = high_sum + moved(split_two(unpacked(recv_buf[s, 0])), from_after)
         for c in range(3):
             advance((c, 0), low_sum[c * 16 : c * 16 + 16])
             advance((c, 4), high_sum[c * 16 : c * 16 + 16])
@@ -341,13 +444,26 @@
             first = ref[c * 80 : c * 80 + 32, :]
             second = ref[c * 80 + 32 : c * 80 + 64, :]
             at = (0 if ref is u_s else 96) + c * 32
-            f_s[at : at + 32, :] = jnp.where(half, first, second)
+            back_out[at : at + 32, :] = jnp.where(half, first, second)
+    if folded:
+
+        @pl.when(away)
+        def _():
+            back = bulk(back_out, back_in, 1, home_id)
+            back.start()
+            back.wait()
+
+        @pl.when(jnp.logical_not(away))
+        def _():
+            back_in[...] = back_out[...]
+
+    final = back_in if folded else back_out
 
     def scatter_step(t, kept):
         here = place_row == t
         new = []
         for k in range(6):
-            row = f_s[pl.ds(k * 32 + t, 1), :]
+            row = final[pl.ds(k * 32 + t, 1), :]
             got = jnp.take_along_axis(
                 jnp.broadcast_to(row, (32, 128)), place_lane, axis=1, mode="promise_in_bounds"
             )
@@ -369,30 +485,34 @@
     operator = jnp.asarray(element_operator())
     nodes = displacement.shape[1]
     vmem = pl.BlockSpec(memory_space=pltpu.VMEM)
+    hbm = pl.BlockSpec(memory_space=pltpu.HBM)
     shape = jax.ShapeDtypeStruct((3, nodes), f32)
     V, S = pltpu.VMEM, pltpu.SemaphoreType.DMA
+    operands = (
+        displacement, velocity, inverse_mass.reshape(32, 128),
+        levels.reshape(1, 64), first_lame.reshape(1, 64), shear_modulus.reshape(1, 64),
+        connectivity.T, owner_list.reshape(4, 128), operator,
+    )
+    folded = lax.axis_size("dom") == 8 and lax.axis_size("lvl") == 4
     return pl.pallas_call(
-        kernel,
+        functools.partial(kernel, folded),
         out_shape=(shape, shape),
-        in_specs=[vmem] * 9,
+        in_specs=[hbm] * 9,
         out_specs=(vmem, vmem),
-        scratch_shapes=[
-            V((125, 128), jnp.int32), V((128, 128), f32), V((32, 128), jnp.int32),
+        scratch_shapes=[V(x.shape, x.dtype) for x in operands] + [S((9,))] + [
+            V((128, 128), f32), V((128, 128), f32), V((32, 128), jnp.int32),
             V((64, 4096), bf16), V((128, 4096), bf16),
             V((256, 128), f32), V((256, 128), f32), V((80, 128), f32), V((256, 128), f32),
             V((2 * TOTAL, 128), bf16), V((8, 128), f32),
+            V((ROWS, 128), f32), V((ROWS, 128), f32), V((192, 128), f32), V((192, 128), f32),
             V((120, 128), f32), V((120, 128), f32), V((8, 128), f32), V((8, 128), f32),
-            V((substeps, 2, 48, 128), f32), V((substeps, 2, 48, 128), f32),
-            S((2,)), S((2,)), S((substeps, 2)), S((substeps, 2)),
+            V((substeps, 2, 24, 128), f32), V((substeps, 2, 24, 128), f32),
+            S((2,)), S((2,)), S((substeps, 2)), S((substeps, 2)), S((2,)), S((2,)),
         ],
         compiler_params=pltpu.CompilerParams(
-            collective_id=0, has_side_effects=True, vmem_limit_bytes=32 * 1024 * 1024
+            collective_id=0, has_side_effects=True, vmem_limit_bytes=63 * 1024 * 1024
         ),
-    )(
-        displacement, velocity, inverse_mass.reshape(32, 128),
-        levels.reshape(1, 64), first_lame.reshape(1, 64), shear_modulus.reshape(1, 64),
-        connectivity, owner_list.reshape(4, 128), operator,
-    )
+    )(*operands)
 
 
 def solution(mesh):

time: 66.4 us -> 53.9 us (0.81)
  Pallas kernels: 56.9 us -> 50 us
  local copies, waits for them, and re-layouts: 8.43 us -> 2.96 us
    pallas_call x1, Pallas kernels: 56.9 us -> 50 us  [per_device(): pl.pallas_call(functools.partial(kernel, folded), out_shape=(shape, shape...]
    unnamed x19 -> x2, local copies, waits for them, and re-layouts: 8.43 us -> 2.96 us
where the time goes in v1:
time: 53.9 us; the launch traced here: 53.6 us
  Pallas kernels  50 us (93%)
  local copies, waits for them, and re-layouts  2.96 us (5%)
  between operations  0.64 us (1%)
    pallas_call x1, Pallas kernels, per_device(): pl.pallas_call(functools.partial(kernel, folded), out_shape=(shape, shape...  50 us
    unnamed x2, local copies, waits for them, and re-layouts  2.96 us

profile of v1, /device:TPU:0, one launch (start us, length us, event | category | flops | bytes accessed | tf_op | source)
XLA Modules:
  0.0 53.6 jit_solution(16635400273128593438)
XLA Ops:
  0.6 50.0 %shard_map.104 = (f32[3,4096]{1,0:T(4,128)}, f32[3,4096]{1,0:T(4,128)}) custom-call(f32[3,4096]{1,0:T(4,128)} %disp_hbm.1, f32[3,4096]{1,0:T(4,128)} %vel_hbm.1, f32[32,128]{1,0:T(8,128)} %bitcast.7, s32[1,64]{1,0:T(1,128)} %bitcast.9, f32[1,64]{1,0:T(1,128)} %bitcast.10, f32[1,64]{1,0:T(1,128)} %bitcast.11, s32[64,125]{1,0:T(8,128)} %bitcast.6, ...), custom_call_target="tpu_custom_call" | custom-call | tf_op jit(solution)/shard_map/pallas_call | solution.py:497
  50.7 1.5 %copy.13 = f32[3,4096]{1,0:T(4,128)} copy(f32[3,4096]{1,0:T(4,128)} %get-tuple-element.4) | data formatting | bytes 98304
  52.2 1.5 %copy.14 = f32[3,4096]{1,0:T(4,128)} copy(f32[3,4096]{1,0:T(4,128)} %get-tuple-element.5) | data formatting | bytes 98304

commit v2 on v1

--- a/solution.py
+++ b/solution.py
@@ -20,8 +20,9 @@
 )
 CENTRE = BLOCK.index((2, 2))
 HIGH = [(4, 0), (4, 1), (4, 2), (4, 3), (1, 4), (2, 4), (3, 4), (0, 4)]
-PLANES = [(c, a) for c in range(3) for a in range(5)]
+PLANES = [(c, a) for a in (0, 4) for c in range(3)] + [(c, a) for c in range(3) for a in (1, 2, 3)]
 MAIN, FACE, TOTAL = 240, 120, 384
+SHARED, OUTER, INNER = 6, 160, 240
 
 
 def lobatto_tables():
@@ -57,20 +58,26 @@
             lame[c, :, a, :] += along[c].T @ (weight[:, None] * along[a])
             shear[c, :, c, :] += along[a].T @ (weight[:, None] * along[a])
             shear[c, :, a, :] += along[a].T @ (weight[:, None] * along[c])
-    rows = []
-    for c, a in PLANES:
-        rows += [c * 125 + a * 25 + b * 5 + k for b, k in BLOCK]
-    for c, a in PLANES:
-        rows += [c * 125 + a * 25 + b * 5 + k for b, k in HIGH]
-    for c, a in PLANES:
-        rows.append(c * 125 + a * 25 + 24)
-    rows = np.array(rows)
-    full = np.zeros((TOTAL, 2 * TOTAL))
-    full[: len(rows), : len(rows)] = lame.reshape(375, 375)[np.ix_(rows, rows)]
-    full[: len(rows), TOTAL : TOTAL + len(rows)] = shear.reshape(375, 375)[np.ix_(rows, rows)]
-    high = full.astype(jnp.bfloat16)
-    low = (full - high.astype(np.float64)).astype(jnp.bfloat16)
-    return np.concatenate([high, low], axis=0)
+
+    def ordered(planes):
+        rows = [c * 125 + a * 25 + b * 5 + k for c, a in planes for b, k in BLOCK]
+        rows += [c * 125 + a * 25 + b * 5 + k for c, a in planes for b, k in HIGH]
+        return np.array(rows + [c * 125 + a * 25 + 24 for c, a in planes])
+
+    taken = ordered(PLANES)
+    parts = []
+    for planes, size in ((PLANES[:SHARED], OUTER), (PLANES[SHARED:], INNER)):
+        given = ordered(planes)
+        part = np.zeros((size, 2 * TOTAL))
+        part[: len(given), : len(taken)] = lame.reshape(375, 375)[np.ix_(given, taken)]
+        part[: len(given), TOTAL : TOTAL + len(taken)] = shear.reshape(375, 375)[np.ix_(given, taken)]
+        high = part.astype(jnp.bfloat16)
+        parts += [high, (part - high.astype(np.float64)).astype(jnp.bfloat16)]
+    return np.concatenate(parts, axis=0)
+
+
+def block_at(c, a):
+    return PLANES.index((c, a)) * 16
 
 
 def node_row(a, b, c):
@@ -115,7 +122,7 @@
     return jnp.where(column == row, 1.0, 0.0).astype(bf16)
 
 
-FOLDED = [5, 1, 3, 2, 0, 4, 6, 7, 11, 10, 8, 12, 14, 15, 13, 9]
+FOLDED = [5, 1, 3, 2, 0, 4, 6, 7, 11, 10, 14, 15, 13, 12, 8, 9]
 STATE, NAMED, ROWS = 224, 232, 240
 
 
@@ -128,7 +135,7 @@
 
 def kernel(
     folded, disp_hbm, vel_hbm, mass_hbm, level_hbm, lame_hbm, shear_hbm, conn_hbm, owner_hbm, oper_hbm,
-    out_u_ref, out_v_ref,
+    final_ref, place_ref,
     disp_ref, vel_ref, mass_ref, level_ref, lame_ref, shear_ref, conn_ref, owner_ref, oper_ref, load_sem,
     conn_s, tile_s, pick_s, hot_hi, hot_lo, u_s, v_s, m_s, f_s, x_s, elem_s,
     pack_out, pack_in, back_out, back_in,
@@ -153,26 +160,31 @@
     def device(index):
         return (index // lvl_size, lax.rem(index, lvl_size))
 
+    def step(index, distance):
+        return lax.rem(index + count + distance, count)
+
     if folded:
-        chips = count // 2
-        chip, core = me // 2, lax.rem(me, 2)
-        order = [FOLDED.index(k) for k in range(chips)]
-        host = looked_up(chip, FOLDED) * 2 + core
-        home = looked_up(chip, order) * 2 + core
-        after_chip = looked_up(chip, [FOLDED[(k + 1) % chips] for k in order])
-        before_chip = looked_up(chip, [FOLDED[k - 1] for k in order])
-        after = jnp.where(core == 1, after_chip * 2, me + 1)
-        before = jnp.where(core == 1, me - 1, before_chip * 2 + 1)
+        order = [FOLDED.index(k) for k in range(count // 2)]
+
+        def host_of(index):
+            return looked_up(index // 2, FOLDED) * 2 + lax.rem(index, 2)
+
+        home = looked_up(me // 2, order) * 2 + lax.rem(me, 2)
+        host = host_of(me)
+        away = host != me
+        after, before = host_of(step(home, 1)), host_of(step(home, -1))
+        low_to, name_to = host_of(step(me, -1)), host_of(step(me, 1))
+        peers = [after, before, low_to, name_to, step(home, 1), step(home, -1)]
         host_id, home_id = device(host), device(home)
-        away = host != me
     else:
-        after = lax.rem(me + 1, count)
-        before = lax.rem(me + count - 1, count)
+        after, before = step(me, 1), step(me, -1)
+        low_to, name_to = before, after
+        peers = [after, before]
     after_id, before_id = device(after), device(before)
 
     barrier = pltpu.get_barrier_semaphore()
-    for other in (after_id, before_id):
-        pl.semaphore_signal(barrier, inc=1, device_id=other, device_id_type=MESH)
+    for other in peers:
+        pl.semaphore_signal(barrier, inc=1, device_id=device(other), device_id_type=MESH)
     if folded:
 
         @pl.when(away)
@@ -243,18 +255,37 @@
         for at in (0, 64):
             pack_out[NAMED + k : NAMED + k + 1, at : at + 64] = ref[...].astype(f32)
 
+    half16 = lanes((16, 128)) < 64
+    for k in range(4):
+        other = got[min(2 * k + 1, 6)][0:16]
+        low_out[k * 16 : k * 16 + 16, :] = jnp.where(
+            half16, got[2 * k][0:16], pltpu.roll(other, 64, axis=1)
+        )
+    low_out[64:72, :] = jnp.broadcast_to(slot_low, (8, 128))
+    owned = float(disp_ref.shape[1])
+    name_out[...] = jnp.broadcast_to(conn_s[NAMES[7] : NAMES[7] + 1, :] - owned, (8, 128))
+    low_copy = pltpu.make_async_remote_copy(
+        src_ref=low_out, dst_ref=low_in, send_sem=init_send.at[0], recv_sem=init_recv.at[0],
+        device_id=device(low_to), device_id_type=MESH,
+    )
+    name_copy = pltpu.make_async_remote_copy(
+        src_ref=name_out, dst_ref=name_in, send_sem=init_send.at[1], recv_sem=init_recv.at[1],
+        device_id=device(name_to), device_id_type=MESH,
+    )
     if folded:
 
         @pl.when(away)
         def _():
-            pl.semaphore_wait(barrier, 4)
+            pl.semaphore_wait(barrier, 8)
             bulk(pack_out, pack_in, 0, host_id).start()
 
         @pl.when(jnp.logical_not(away))
         def _():
-            pl.semaphore_wait(barrier, 2)
+            pl.semaphore_wait(barrier, 6)
     else:
         pl.semaphore_wait(barrier, 2)
+    low_copy.start()
+    name_copy.start()
 
     def find_places():
         for r in range(32):
@@ -268,8 +299,10 @@
         )
         return place[0:32].astype(jnp.int32), place[32:64].astype(jnp.int32)
 
+    place_lane, place_row = find_places()
+    place_ref[0:32, :] = place_lane
+    place_ref[32:64, :] = place_row
     if folded:
-        place_lane, place_row = find_places()
 
         @pl.when(away)
         def _():
@@ -283,33 +316,16 @@
     for k, ref in enumerate([u_s] * 3 + [v_s] * 3 + [m_s]):
         packed = held[k * 32 : k * 32 + 32, :]
         turned = pltpu.roll(packed, 64, axis=1)
-        base = (k % 3) * 80 if k < 6 else 0
-        ref[base : base + 32, :] = jnp.where(half, packed, turned)
-        ref[base + 32 : base + 64, :] = jnp.where(half, turned, packed)
+        low, high = jnp.where(half, packed, turned), jnp.where(half, turned, packed)
+        for a in range(4):
+            at = block_at(k % 3, a) if k < 6 else a * 16
+            ref[at : at + 16, :] = (low if a < 2 else high)[a % 2 * 16 : a % 2 * 16 + 16]
     u_s[MAIN : MAIN + 16, :] = jnp.zeros((16, 128), f32)
     f_s[MAIN : MAIN + 16, :] = jnp.zeros((16, 128), f32)
     elem_s[...] = held[NAMED : NAMED + 8, :]
     slot_low = elem_s[0:1, :]
     name_row = [held[STATE + k : STATE + k + 1, :] for k in range(8)]
-    owned = float(disp_ref.shape[1])
     slot_high = name_row[7] - owned
-
-    for k in range(3):
-        low_out[k * 16 : k * 16 + 16, :] = u_s[k * 80 : k * 80 + 16, :]
-        low_out[48 + k * 16 : 64 + k * 16, :] = v_s[k * 80 : k * 80 + 16, :]
-    low_out[96:112, :] = m_s[0:16, :]
-    low_out[112:120, :] = jnp.broadcast_to(slot_low, (8, 128))
-    name_out[...] = jnp.broadcast_to(slot_high, (8, 128))
-    low_copy = pltpu.make_async_remote_copy(
-        src_ref=low_out, dst_ref=low_in, send_sem=init_send.at[0], recv_sem=init_recv.at[0],
-        device_id=before_id, device_id_type=MESH,
-    )
-    name_copy = pltpu.make_async_remote_copy(
-        src_ref=name_out, dst_ref=name_in, send_sem=init_send.at[1], recv_sem=init_recv.at[1],
-        device_id=after_id, device_id_type=MESH,
-    )
-    low_copy.start()
-    name_copy.start()
 
     tile_s[0:8, :] = held[STATE : STATE + 8, :]
     columns = jnp.transpose(tile_s[...])
@@ -326,36 +342,69 @@
     collect_edge = same(name_col[5], name_row[4])
     to_high = same(name_col[6], name_row[7])
     to_low = same(name_col[7], name_row[6])
-    if not folded:
-        place_lane, place_row = find_places()
 
     low_copy.wait()
     name_copy.wait()
-    tile_s[0:8, :] = low_in[112:120, :]
+    tile_s[0:8, :] = low_in[64:72, :]
     tile_s[8:16, :] = name_in[...]
     columns = jnp.transpose(tile_s[...])
     from_after = same(columns[:, 0:1], slot_high)
     from_before = same(columns[:, 8:9], slot_low)
     to_high_twice = jnp.concatenate([to_high, to_high], axis=0)
     from_after_twice = jnp.concatenate([from_after, from_after], axis=0)
-    high = moved(split_three(low_out[0:112, :]), to_high_twice)
-    high = high + moved(split_three(low_in[0:112, :]), from_after_twice)
-    for k in range(3):
-        u_s[k * 80 + 64 : k * 80 + 80, :] = high[k * 16 : k * 16 + 16]
-        v_s[k * 80 + 64 : k * 80 + 80, :] = high[48 + k * 16 : 64 + k * 16]
+    theirs = []
+    for k in range(7):
+        packed = low_in[k // 2 * 16 : k // 2 * 16 + 16, :]
+        turned = pltpu.roll(packed, 64, axis=1)
+        theirs.append(jnp.where(half16 if k % 2 == 0 else jnp.logical_not(half16), packed, turned))
+    ours = jnp.concatenate([u_s[0:48, :], v_s[0:48, :], m_s[0:16, :]], axis=0)
+    high = moved(split_three(ours), to_high_twice)
+    high = high + moved(split_three(jnp.concatenate(theirs, axis=0)), from_after_twice)
+    u_s[48:96, :] = high[0:48]
+    v_s[48:96, :] = high[48:96]
     m_s[64:80, :] = high[96:112]
     loads[8].wait()
 
     level = elem_s[1:2, :]
     period = jnp.where(level == 0.0, 8, jnp.where(level == 1.0, 4, jnp.where(level == 2.0, 2, 1)))
     row8 = sublanes((15, 8, 128))
-
-    def advance(rows, force):
-        c_rows = pl.ds(rows[0] * 80 + rows[1] * 16, 16)
-        mass = m_s[pl.ds(rows[1] * 16, 16), :]
-        speed = v_s[c_rows, :] - substep_length * mass * force
-        v_s[c_rows, :] = speed
-        u_s[c_rows, :] = u_s[c_rows, :] + substep_length * speed
+    row16 = sublanes((16, 128))
+    in_first = (row16 == 0) | (row16 == 3) | ((row16 >= 6) & (row16 < 9))
+    in_second = (row16 == 1) | (row16 == 4) | ((row16 >= 9) & (row16 < 12))
+    half24 = lanes((24, 128)) < 64
+
+    def advance(first, size, mass, force):
+        rows = pl.ds(first, size)
+        speed = v_s[rows, :] - substep_length * mass * force
+        v_s[rows, :] = speed
+        u_s[rows, :] = u_s[rows, :] + substep_length * speed
+
+    def mass_of(first, size):
+        one = m_s[first : first + size, :]
+        return jnp.concatenate([one, one, one], axis=0)
+
+    def summed(product, size, planes, first):
+        force = product[0:size] + product[size : 2 * size]
+        force = force + pltpu.roll(force, 64, axis=1)
+        main, faces = planes * 16, planes * 24
+        moved_face = moved(split_two(force[main:faces]), collect)
+        along_y = moved_face[:, 0:128].reshape(planes, 8, 128)
+        along_z = moved_face[:, 128:256].reshape(planes, 8, 128)
+        row = row8[0:planes]
+        low = jnp.where(row < 4, along_y, jnp.where(row < 7, along_z, 0.0))
+        low = low + jnp.where(row == 0, pltpu.roll(along_z, 1, axis=1), 0.0)
+        both = force[0:main].reshape(planes, 2, 8, 128)
+        both = jnp.concatenate([both[:, 0:1] + low[:, None], both[:, 1:2]], axis=1)
+        f_s[first : first + main, :] = both.reshape(main, 128)
+        edge = moved(split_two(force[faces:size]), collect_edge)[0:planes]
+        at = pl.ds(first, planes, stride=16)
+        f_s[at, :] = f_s[at, :] + edge
+
+    def unpacked(packed):
+        turned = pltpu.roll(packed, 64, axis=1)
+        return jnp.concatenate(
+            [jnp.where(half24, packed, turned), jnp.where(half24, turned, packed)], axis=0
+        )
 
     def substep(s, carry):
         u = u_s[0:MAIN, :].reshape(15, 16, 128)
@@ -366,44 +415,24 @@
             row8 < 4, along_y, jnp.where(row8 < 7, along_z, pltpu.roll(along_z, 7, axis=1))
         )
         edge = moved(split_three(u_s[pl.ds(0, 16, stride=16), :]), spread_edge)
-        centres = [
-            u_s[c * 80 + 32 + CENTRE : c * 80 + 33 + CENTRE, :] for c in range(3)
-        ]
-        row16 = sublanes((16, 128))
-        edge = edge - jnp.where(
-            row16 < 5, centres[0], jnp.where(row16 < 10, centres[1], centres[2])
-        )
+        centres = []
+        for c in range(3):
+            at = block_at(c, 2) + CENTRE
+            centres.append(u_s[at : at + 1, :])
+        edge = edge - jnp.where(in_first, centres[0], jnp.where(in_second, centres[1], centres[2]))
         edge = jnp.where(row16 < 15, edge, 0.0)
         active = lax.rem(jnp.full((1, 128), s, jnp.int32), period) == 0
         weight = jnp.where(active, period.astype(f32), 0.0)
-        for part, value in enumerate((elem_s[2:3, :] * weight, elem_s[3:4, :] * weight)):
-            at = part * TOTAL
-            for c in range(3):
-                main = (u[c * 5 : c * 5 + 5].reshape(80, 128) - centres[c]) * value
-                x_s[at + c * 80 : at + c * 80 + 80, :] = split_two(main)
-            both = [
-                (face[c * 5 : c * 5 + 5].reshape(40, 128) - centres[c]) * value for c in range(3)
-            ]
-            both += [edge * value, jnp.zeros((8, 128), f32)]
-            x_s[at + MAIN : at + TOTAL, :] = split_two(jnp.concatenate(both, axis=0))
-        product = jnp.dot(oper_ref[...], x_s[...], preferred_element_type=f32)
-        force = product[0:TOTAL] + product[TOTAL : 2 * TOTAL]
-        force = force + pltpu.roll(force, 64, axis=1)
-
-        face = moved(split_two(force[MAIN : MAIN + FACE]), collect)
-        along_y = face[:, 0:128].reshape(15, 8, 128)
-        along_z = face[:, 128:256].reshape(15, 8, 128)
-        low = jnp.where(row8 < 4, along_y, jnp.where(row8 < 7, along_z, 0.0))
-        low = low + jnp.where(row8 == 0, pltpu.roll(along_z, 1, axis=1), 0.0)
-        main = force[0:MAIN].reshape(15, 2, 8, 128)
-        main = jnp.concatenate([main[:, 0:1] + low[:, None], main[:, 1:2]], axis=1)
-        f_s[0:MAIN, :] = main.reshape(MAIN, 128)
-        edge = moved(split_two(force[MAIN + FACE : MAIN + FACE + 16]), collect_edge)
-        f_s[pl.ds(0, 16, stride=16), :] = f_s[pl.ds(0, 16, stride=16), :] + edge
-
-        low_x = jnp.concatenate([f_s[c * 80 : c * 80 + 16, :] for c in range(3)], axis=0)
-        high_x = jnp.concatenate([f_s[c * 80 + 64 : c * 80 + 80, :] for c in range(3)], axis=0)
-        half24 = lanes((24, 128)) < 64
+        main = [u[k] - centres[c] for k, (c, _) in enumerate(PLANES)]
+        face = [face[k] - centres[c] for k, (c, _) in enumerate(PLANES)]
+        values = jnp.concatenate(main + face + [edge, jnp.zeros((8, 128), f32)], axis=0)
+        x_s[0:TOTAL, :] = split_two(values * (elem_s[2:3, :] * weight))
+        x_s[TOTAL : 2 * TOTAL, :] = split_two(values * (elem_s[3:4, :] * weight))
+
+        x = x_s[...]
+        product = jnp.dot(oper_ref[0 : 2 * OUTER, :], x, preferred_element_type=f32)
+        summed(product, OUTER, SHARED, 0)
+        low_x, high_x = f_s[0:48, :], f_s[48:96, :]
         send_buf[s, 0] = jnp.where(half24, low_x[0:24], low_x[24:48])
         send_buf[s, 1] = jnp.where(half24, high_x[0:24], high_x[24:48])
         copies = [
@@ -416,35 +445,29 @@
         ]
         copies[1].start()
         copies[0].start()
+        product = jnp.dot(oper_ref[2 * OUTER :, :], x, preferred_element_type=f32)
+        summed(product, INNER, 15 - SHARED, 96)
         low_sum = low_x + moved(split_two(high_x), to_low)
         high_sum = high_x + moved(split_two(low_x), to_high)
-        for c in range(3):
-            for a in (1, 2, 3):
-                advance((c, a), f_s[c * 80 + a * 16 : c * 80 + a * 16 + 16, :])
+        advance(96, 144, mass_of(16, 48), f_s[96:240, :])
         copies[1].wait()
         copies[0].wait()
-
-        def unpacked(packed):
-            turned = pltpu.roll(packed, 64, axis=1)
-            return jnp.concatenate(
-                [jnp.where(half24, packed, turned), jnp.where(half24, turned, packed)], axis=0
-            )
-
         low_sum = low_sum + moved(split_two(unpacked(recv_buf[s, 1])), from_before)
         high_sum = high_sum + moved(split_two(unpacked(recv_buf[s, 0])), from_after)
-        for c in range(3):
-            advance((c, 0), low_sum[c * 16 : c * 16 + 16])
-            advance((c, 4), high_sum[c * 16 : c * 16 + 16])
+        advance(0, 48, mass_of(0, 16), low_sum)
+        advance(48, 48, mass_of(64, 16), high_sum)
         return carry
 
     lax.fori_loop(0, substeps, substep, 0)
 
     for ref in (u_s, v_s):
         for c in range(3):
-            first = ref[c * 80 : c * 80 + 32, :]
-            second = ref[c * 80 + 32 : c * 80 + 64, :]
             at = (0 if ref is u_s else 96) + c * 32
-            back_out[at : at + 32, :] = jnp.where(half, first, second)
+            for a in range(2):
+                one, two = block_at(c, a), block_at(c, a + 2)
+                back_out[at + a * 16 : at + a * 16 + 16, :] = jnp.where(
+                    half16, ref[one : one + 16, :], ref[two : two + 16, :]
+                )
     if folded:
 
         @pl.when(away)
@@ -457,13 +480,17 @@
         def _():
             back_in[...] = back_out[...]
 
-    final = back_in if folded else back_out
+    final_ref[...] = (back_in if folded else back_out)[...]
+
+
+def reorder(final_ref, place_ref, out_u_ref, out_v_ref):
+    place_lane, place_row = place_ref[0:32, :], place_ref[32:64, :]
 
     def scatter_step(t, kept):
         here = place_row == t
         new = []
         for k in range(6):
-            row = final[pl.ds(k * 32 + t, 1), :]
+            row = final_ref[pl.ds(k * 32 + t, 1), :]
             got = jnp.take_along_axis(
                 jnp.broadcast_to(row, (32, 128)), place_lane, axis=1, mode="promise_in_bounds"
             )
@@ -494,9 +521,10 @@
         connectivity.T, owner_list.reshape(4, 128), operator,
     )
     folded = lax.axis_size("dom") == 8 and lax.axis_size("lvl") == 4
-    return pl.pallas_call(
+    held = (jax.ShapeDtypeStruct((192, 128), f32), jax.ShapeDtypeStruct((64, 128), jnp.int32))
+    final, place = pl.pallas_call(
         functools.partial(kernel, folded),
-        out_shape=(shape, shape),
+        out_shape=held,
         in_specs=[hbm] * 9,
         out_specs=(vmem, vmem),
         scratch_shapes=[V(x.shape, x.dtype) for x in operands] + [S((9,))] + [
@@ -505,7 +533,7 @@
             V((256, 128), f32), V((256, 128), f32), V((80, 128), f32), V((256, 128), f32),
             V((2 * TOTAL, 128), bf16), V((8, 128), f32),
             V((ROWS, 128), f32), V((ROWS, 128), f32), V((192, 128), f32), V((192, 128), f32),
-            V((120, 128), f32), V((120, 128), f32), V((8, 128), f32), V((8, 128), f32),
+            V((72, 128), f32), V((72, 128), f32), V((8, 128), f32), V((8, 128), f32),
             V((substeps, 2, 24, 128), f32), V((substeps, 2, 24, 128), f32),
             S((2,)), S((2,)), S((substeps, 2)), S((substeps, 2)), S((2,)), S((2,)),
         ],
@@ -513,6 +541,13 @@
             collective_id=0, has_side_effects=True, vmem_limit_bytes=63 * 1024 * 1024
         ),
     )(*operands)
+    return pl.pallas_call(
+        reorder,
+        out_shape=(shape, shape),
+        in_specs=[vmem] * 2,
+        out_specs=(vmem, vmem),
+        compiler_params=pltpu.CompilerParams(vmem_limit_bytes=63 * 1024 * 1024),
+    )(final, place)
 
 
 def solution(mesh):

time: 53.9 us -> 50.5 us (0.937)
  local copies, waits for them, and re-layouts: 2.96 us -> 0 us
    unnamed x2 -> x0, local copies, waits for them, and re-layouts: 2.96 us -> none
    pallas_call x1 -> x2, Pallas kernels: 50 us -> 49.6 us  [the longest x1 45.4 us: per_device(): pl.pallas_call(functools.partial(kernel, folded), out_shape=held, in_spec...]
where the time goes in v2:
time: 50.5 us; the launch traced here: 50.3 us
  Pallas kernels  49.6 us (98%)
  between operations  0.64 us (1%)
    pallas_call x1, Pallas kernels, per_device(): pl.pallas_call(functools.partial(kernel, folded), out_shape=held, in_spec...  45.4 us
    pallas_call x1, Pallas kernels, per_device(): pl.pallas_call(reorder, out_shape=(shape, shape), in_specs=[vmem] * 2, ou...  4.24 us

profile of v2, /device:TPU:0, one launch (start us, length us, event | category | flops | bytes accessed | tf_op | source)
XLA Modules:
  0.0 50.3 jit_solution(10400678844937103256)
XLA Ops:
  0.6 45.4 %shard_map.104 = (f32[192,128]{1,0:T(8,128)}, s32[64,128]{1,0:T(8,128)}) custom-call(f32[3,4096]{1,0:T(4,128)} %disp_hbm.1, f32[3,4096]{1,0:T(4,128)} %vel_hbm.1, f32[32,128]{1,0:T(8,128)} %bitcast.7, s32[1,64]{1,0:T(1,128)} %bitcast.9, f32[1,64]{1,0:T(1,128)} %bitcast.10, f32[1,64]{1,0:T(1,128)} %bitcast.11, s32[64,125]{1,0:T(8,128)} %bitcast.6, ...), custom_call_target="tpu_custom_call" | custom-call | tf_op jit(solution)/shard_map/pallas_call | solution.py:525
  46.0 4.2 %shard_map.105 = (f32[3,4096]{1,0:T(4,128)}, f32[3,4096]{1,0:T(4,128)}) custom-call(f32[192,128]{1,0:T(8,128)} %get-tuple-element.4.final_ref, s32[64,128]{1,0:T(8,128)} %get-tuple-element.5.place_ref), custom_call_target="tpu_custom_call" | custom-call | tf_op jit(solution)/shard_map/pallas_call | solution.py:544

commit v3 on v2

--- a/solution.py
+++ b/solution.py
@@ -22,7 +22,7 @@
 HIGH = [(4, 0), (4, 1), (4, 2), (4, 3), (1, 4), (2, 4), (3, 4), (0, 4)]
 PLANES = [(c, a) for a in (0, 4) for c in range(3)] + [(c, a) for c in range(3) for a in (1, 2, 3)]
 MAIN, FACE, TOTAL = 240, 120, 384
-SHARED, OUTER, INNER = 6, 160, 240
+SHARED, OUTER, INNER, DELTA = 6, 160, 240, 192
 
 
 def lobatto_tables():
@@ -65,12 +65,16 @@
         return np.array(rows + [c * 125 + a * 25 + 24 for c, a in planes])
 
     taken = ordered(PLANES)
+    shared = ordered(PLANES[:SHARED])
+    spots = np.concatenate([np.arange(SHARED * 24), SHARED * 24 + 8 * np.arange(SHARED)])
     parts = []
     for planes, size in ((PLANES[:SHARED], OUTER), (PLANES[SHARED:], INNER)):
         given = ordered(planes)
-        part = np.zeros((size, 2 * TOTAL))
-        part[: len(given), : len(taken)] = lame.reshape(375, 375)[np.ix_(given, taken)]
-        part[: len(given), TOTAL : TOTAL + len(taken)] = shear.reshape(375, 375)[np.ix_(given, taken)]
+        part = np.zeros((size, 2 * TOTAL + 2 * DELTA))
+        for k, table in enumerate((lame.reshape(375, 375), shear.reshape(375, 375))):
+            part[: len(given), k * TOTAL : k * TOTAL + len(taken)] = table[np.ix_(given, taken)]
+            at = 2 * TOTAL + k * DELTA
+            part[: len(given), at + spots] = table[np.ix_(given, shared)]
         high = part.astype(jnp.bfloat16)
         parts += [high, (part - high.astype(np.float64)).astype(jnp.bfloat16)]
     return np.concatenate(parts, axis=0)
@@ -123,7 +127,7 @@
 
 
 FOLDED = [5, 1, 3, 2, 0, 4, 6, 7, 11, 10, 14, 15, 13, 12, 8, 9]
-STATE, NAMED, ROWS = 224, 232, 240
+NAMES_AT, PARAMS_AT, SPEED_AT, MASS_AT, ROWS = 96, 104, 112, 208, 240
 
 
 def looked_up(index, table):
@@ -137,7 +141,7 @@
     folded, disp_hbm, vel_hbm, mass_hbm, level_hbm, lame_hbm, shear_hbm, conn_hbm, owner_hbm, oper_hbm,
     final_ref, place_ref,
     disp_ref, vel_ref, mass_ref, level_ref, lame_ref, shear_ref, conn_ref, owner_ref, oper_ref, load_sem,
-    conn_s, tile_s, pick_s, hot_hi, hot_lo, u_s, v_s, m_s, f_s, x_s, elem_s,
+    conn_s, tile_s, pick_s, hot_hi, hot_lo, u_s, v_s, m_s, f_s, x_s, elem_s, known_s, change_s, rate_s,
     pack_out, pack_in, back_out, back_in,
     low_out, low_in, name_out, name_in, send_buf, recv_buf,
     init_send, init_recv, step_send, step_recv, bulk_send, bulk_recv,
@@ -214,32 +218,32 @@
     pick = pick_s[...]
     pick_hi, pick_lo = lax.shift_right_logical(pick, 7), lax.bitwise_and(pick, 127)
 
+    def gathered(refs, singles):
+        def gather_step(t, kept):
+            here = pick_hi == t
+            cols = pl.ds(pl.multiple_of(t * 128, 128), 128)
+            rows = [ref[c : c + 1, cols] for ref in refs for c in range(3)]
+            rows += [ref[pl.ds(t, 1), :] for ref in singles]
+            new = []
+            for row, old in zip(rows, kept):
+                got = jnp.take_along_axis(
+                    jnp.broadcast_to(row, (32, 128)), pick_lo, axis=1, mode="promise_in_bounds"
+                )
+                new.append(jnp.where(here, got, old))
+            return tuple(new)
+
+        start = tuple(jnp.zeros((32, 128), f32) for _ in range(3 * len(refs) + len(singles)))
+        return list(lax.fori_loop(0, 32, gather_step, start, unroll=4))
+
     for load in loads[1:8]:
         load.wait()
-
-    def gather_step(t, kept):
-        here = pick_hi == t
-        cols = pl.ds(pl.multiple_of(t * 128, 128), 128)
-        rows = [disp_ref[c : c + 1, cols] for c in range(3)]
-        rows += [vel_ref[c : c + 1, cols] for c in range(3)]
-        rows.append(mass_ref[pl.ds(t, 1), :])
-        new = []
-        for row, old in zip(rows, kept):
-            got = jnp.take_along_axis(
-                jnp.broadcast_to(row, (32, 128)), pick_lo, axis=1, mode="promise_in_bounds"
-            )
-            new.append(jnp.where(here, got, old))
-        return tuple(new)
-
-    got = lax.fori_loop(
-        0, 32, gather_step, tuple(jnp.zeros((32, 128), f32) for _ in range(7)), unroll=4
-    )
+    got = gathered([disp_ref], [])
     half = lanes((32, 128)) < 64
-    for k in range(7):
+    for k in range(3):
         pack_out[k * 32 : k * 32 + 32, :] = got[k]
 
     for k, r in enumerate(NAMES):
-        pack_out[STATE + k : STATE + k + 1, :] = conn_s[r : r + 1, :]
+        pack_out[NAMES_AT + k : NAMES_AT + k + 1, :] = conn_s[r : r + 1, :]
     tile_s[0:8, :] = jnp.zeros((8, 128), f32)
     tile_s[0:4, :] = owner_ref[...].astype(f32)
     columns = jnp.transpose(tile_s[...])
@@ -249,11 +253,39 @@
         hit = columns[:, k : k + 1] == low_name
         number = sublanes((128, 128)).astype(f32) + (k * 128 + 9999)
         slot_low = slot_low + jnp.sum(jnp.where(hit, number, 0.0), axis=0, keepdims=True)
-    pack_out[NAMED : NAMED + 8, :] = jnp.zeros((8, 128), f32)
-    pack_out[NAMED : NAMED + 1, :] = slot_low
+    pack_out[PARAMS_AT : PARAMS_AT + 8, :] = jnp.zeros((8, 128), f32)
+    pack_out[PARAMS_AT : PARAMS_AT + 1, :] = slot_low
     for k, ref in enumerate((level_ref, lame_ref, shear_ref), 1):
         for at in (0, 64):
-            pack_out[NAMED + k : NAMED + k + 1, at : at + 64] = ref[...].astype(f32)
+            pack_out[PARAMS_AT + k : PARAMS_AT + k + 1, at : at + 64] = ref[...].astype(f32)
+
+    def first_move():
+        return bulk(pack_out.at[0:SPEED_AT], pack_in.at[0:SPEED_AT], 0, host_id)
+
+    def second_move():
+        return bulk(pack_out.at[SPEED_AT:ROWS], pack_in.at[SPEED_AT:ROWS], 1, host_id)
+
+    if folded:
+
+        @pl.when(away)
+        def _():
+            pl.semaphore_wait(barrier, 8)
+            first_move().start()
+
+        @pl.when(jnp.logical_not(away))
+        def _():
+            pl.semaphore_wait(barrier, 6)
+    else:
+        pl.semaphore_wait(barrier, 2)
+    got = got + gathered([vel_ref], [mass_ref])
+    for k in range(3, 7):
+        at = SPEED_AT + (k - 3) * 32
+        pack_out[at : at + 32, :] = got[k]
+    if folded:
+
+        @pl.when(away)
+        def _():
+            second_move().start()
 
     half16 = lanes((16, 128)) < 64
     for k in range(4):
@@ -272,18 +304,6 @@
         src_ref=name_out, dst_ref=name_in, send_sem=init_send.at[1], recv_sem=init_recv.at[1],
         device_id=device(name_to), device_id_type=MESH,
     )
-    if folded:
-
-        @pl.when(away)
-        def _():
-            pl.semaphore_wait(barrier, 8)
-            bulk(pack_out, pack_in, 0, host_id).start()
-
-        @pl.when(jnp.logical_not(away))
-        def _():
-            pl.semaphore_wait(barrier, 6)
-    else:
-        pl.semaphore_wait(barrier, 2)
     low_copy.start()
     name_copy.start()
 
@@ -306,7 +326,8 @@
 
         @pl.when(away)
         def _():
-            bulk(pack_out, pack_in, 0, host_id).wait()
+            first_move().wait()
+            second_move().wait()
 
         @pl.when(jnp.logical_not(away))
         def _():
@@ -314,7 +335,8 @@
 
     held = pack_in if folded else pack_out
     for k, ref in enumerate([u_s] * 3 + [v_s] * 3 + [m_s]):
-        packed = held[k * 32 : k * 32 + 32, :]
+        at = k * 32 if k < 3 else SPEED_AT + (k - 3) * 32
+        packed = held[at : at + 32, :]
         turned = pltpu.roll(packed, 64, axis=1)
         low, high = jnp.where(half, packed, turned), jnp.where(half, turned, packed)
         for a in range(4):
@@ -322,20 +344,19 @@
             ref[at : at + 16, :] = (low if a < 2 else high)[a % 2 * 16 : a % 2 * 16 + 16]
     u_s[MAIN : MAIN + 16, :] = jnp.zeros((16, 128), f32)
     f_s[MAIN : MAIN + 16, :] = jnp.zeros((16, 128), f32)
-    elem_s[...] = held[NAMED : NAMED + 8, :]
+    elem_s[...] = held[PARAMS_AT : PARAMS_AT + 8, :]
     slot_low = elem_s[0:1, :]
-    name_row = [held[STATE + k : STATE + k + 1, :] for k in range(8)]
+    name_row = [held[NAMES_AT + k : NAMES_AT + k + 1, :] for k in range(8)]
     slot_high = name_row[7] - owned
 
-    tile_s[0:8, :] = held[STATE : STATE + 8, :]
+    tile_s[0:8, :] = held[NAMES_AT : NAMES_AT + 8, :]
     columns = jnp.transpose(tile_s[...])
     name_col = [columns[:, k : k + 1] for k in range(8)]
-    spread = jnp.concatenate(
-        [same(name_col[0], name_row[1]), same(name_col[2], name_row[3])], axis=1
-    )
+    to_y, to_z = same(name_col[0], name_row[1]), same(name_col[2], name_row[3])
+    to_edge = same(name_col[4], name_row[5])
+    spread = jnp.concatenate([to_y, to_z], axis=1)
     spread = jnp.concatenate([spread, spread], axis=0)
-    spread_edge = same(name_col[4], name_row[5])
-    spread_edge = jnp.concatenate([spread_edge, spread_edge], axis=0)
+    spread_edge = jnp.concatenate([to_edge, to_edge], axis=0)
     collect = jnp.concatenate(
         [same(name_col[1], name_row[0]), same(name_col[3], name_row[2])], axis=1
     )
@@ -373,18 +394,37 @@
     in_second = (row16 == 1) | (row16 == 4) | ((row16 >= 9) & (row16 < 12))
     half24 = lanes((24, 128)) < 64
 
+    def face_of(along_y, along_z):
+        row = row8[0 : along_y.shape[0]]
+        turned = pltpu.roll(along_z, 7, axis=1)
+        return jnp.where(row < 4, along_y, jnp.where(row < 7, along_z, turned))
+
+    def passed_on(matrix):
+        onward = jnp.concatenate([to_y, to_z, to_edge], axis=1)
+        return jnp.concatenate([matrix, (0.5 * moved(matrix, onward)).astype(bf16)], axis=1)
+
+    onto_low, onto_high = passed_on(from_before), passed_on(from_after)
+
+    def thrice(x):
+        return jnp.concatenate([x, x, x], axis=0)
+
+    for k, at in enumerate((0, 64)):
+        block = m_s[at : at + 16, :]
+        top = split_three(block[0:8])
+        faces = moved(top, spread)
+        face = face_of(faces[:, 0:128].reshape(1, 8, 128), faces[:, 128:256].reshape(1, 8, 128))
+        edge = moved(top, spread_edge)
+        rate_s[k * 48 : k * 48 + 48, :] = -substep_length * thrice(block)
+        rate_s[96 + k * 24 : 120 + k * 24, :] = -substep_length * thrice(face.reshape(8, 128))
+        rate_s[144 + k * 24 : 168 + k * 24, :] = -substep_length * thrice(edge)
+
     def advance(first, size, mass, force):
         rows = pl.ds(first, size)
         speed = v_s[rows, :] - substep_length * mass * force
         v_s[rows, :] = speed
         u_s[rows, :] = u_s[rows, :] + substep_length * speed
 
-    def mass_of(first, size):
-        one = m_s[first : first + size, :]
-        return jnp.concatenate([one, one, one], axis=0)
-
-    def summed(product, size, planes, first):
-        force = product[0:size] + product[size : 2 * size]
+    def summed(force, planes, first):
         force = force + pltpu.roll(force, 64, axis=1)
         main, faces = planes * 16, planes * 24
         moved_face = moved(split_two(force[main:faces]), collect)
@@ -396,7 +436,7 @@
         both = force[0:main].reshape(planes, 2, 8, 128)
         both = jnp.concatenate([both[:, 0:1] + low[:, None], both[:, 1:2]], axis=1)
         f_s[first : first + main, :] = both.reshape(main, 128)
-        edge = moved(split_two(force[faces:size]), collect_edge)[0:planes]
+        edge = moved(split_two(force[faces:]), collect_edge)[0:planes]
         at = pl.ds(first, planes, stride=16)
         f_s[at, :] = f_s[at, :] + edge
 
@@ -406,14 +446,25 @@
             [jnp.where(half24, packed, turned), jnp.where(half24, turned, packed)], axis=0
         )
 
-    def substep(s, carry):
+    def weights(s):
+        active = lax.rem(jnp.full((1, 128), s, jnp.int32), period) == 0
+        weight = jnp.where(active, period.astype(f32), 0.0)
+        return elem_s[2:3, :] * weight, elem_s[3:4, :] * weight
+
+    def exchange(s):
+        return [
+            pltpu.make_async_remote_copy(
+                src_ref=send_buf.at[s, way], dst_ref=recv_buf.at[s, way],
+                send_sem=step_send.at[s, way], recv_sem=step_recv.at[s, way],
+                device_id=other, device_id_type=MESH,
+            )
+            for way, other in enumerate((before_id, after_id))
+        ]
+
+    def know(s):
         u = u_s[0:MAIN, :].reshape(15, 16, 128)
         faces = moved(split_three(u[:, 0:8].reshape(FACE, 128)), spread)
-        along_y = faces[:, 0:128].reshape(15, 8, 128)
-        along_z = faces[:, 128:256].reshape(15, 8, 128)
-        face = jnp.where(
-            row8 < 4, along_y, jnp.where(row8 < 7, along_z, pltpu.roll(along_z, 7, axis=1))
-        )
+        face = face_of(faces[:, 0:128].reshape(15, 8, 128), faces[:, 128:256].reshape(15, 8, 128))
         edge = moved(split_three(u_s[pl.ds(0, 16, stride=16), :]), spread_edge)
         centres = []
         for c in range(3):
@@ -421,66 +472,107 @@
             centres.append(u_s[at : at + 1, :])
         edge = edge - jnp.where(in_first, centres[0], jnp.where(in_second, centres[1], centres[2]))
         edge = jnp.where(row16 < 15, edge, 0.0)
-        active = lax.rem(jnp.full((1, 128), s, jnp.int32), period) == 0
-        weight = jnp.where(active, period.astype(f32), 0.0)
         main = [u[k] - centres[c] for k, (c, _) in enumerate(PLANES)]
         face = [face[k] - centres[c] for k, (c, _) in enumerate(PLANES)]
         values = jnp.concatenate(main + face + [edge, jnp.zeros((8, 128), f32)], axis=0)
-        x_s[0:TOTAL, :] = split_two(values * (elem_s[2:3, :] * weight))
-        x_s[TOTAL : 2 * TOTAL, :] = split_two(values * (elem_s[3:4, :] * weight))
-
+        for k, weight in enumerate(weights(s)):
+            x_s[k * TOTAL : (k + 1) * TOTAL, :] = split_two(values * weight)
         x = x_s[...]
-        product = jnp.dot(oper_ref[0 : 2 * OUTER, :], x, preferred_element_type=f32)
-        summed(product, OUTER, SHARED, 0)
+        for first, size in ((0, OUTER), (OUTER, INNER)):
+            rows = slice(2 * first, 2 * (first + size))
+            product = jnp.dot(oper_ref[rows, 0 : 2 * TOTAL], x, preferred_element_type=f32)
+            known_s[first : first + size, :] = product[0:size] + product[size:]
+
+    def arrived(s):
+        for copy in exchange(s)[::-1]:
+            copy.wait()
+        both = [
+            moved(split_two(unpacked(recv_buf[s, way])), matrix)
+            for way, matrix in ((1, onto_low), (0, onto_high))
+        ]
+        main = jnp.concatenate([x[:, 0:128] for x in both], axis=0) * rate_s[0:96, :]
+        v_s[0:96, :] = v_s[0:96, :] + main
+        main = substep_length * main
+        u_s[0:96, :] = u_s[0:96, :] + main
+        tops = [
+            jnp.concatenate(
+                [x[:, k * 128 : k * 128 + 128].reshape(3, 16, 128)[:, 0:8] for x in both], axis=0
+            )
+            for k in (1, 2, 3)
+        ]
+        rest = jnp.concatenate(
+            [face_of(tops[0], tops[1]).reshape(48, 128), tops[2].reshape(48, 128)], axis=0
+        )
+        return jnp.concatenate([main, substep_length * rest * rate_s[96:192, :]], axis=0)
+
+    def changed(first, size):
+        rows = slice(2 * first, 2 * (first + size))
+        product = jnp.dot(oper_ref[rows, 2 * TOTAL :], change_s[...], preferred_element_type=f32)
+        return product[0:size] + product[size:]
+
+    def substep(s, follow):
+        if follow:
+            change = arrived(s - 1)
+            for k, weight in enumerate(weights(s)):
+                change_s[k * DELTA : (k + 1) * DELTA, :] = split_two(change * weight)
+        force = known_s[0:OUTER, :]
+        summed(force + changed(0, OUTER) if follow else force, SHARED, 0)
         low_x, high_x = f_s[0:48, :], f_s[48:96, :]
         send_buf[s, 0] = jnp.where(half24, low_x[0:24], low_x[24:48])
         send_buf[s, 1] = jnp.where(half24, high_x[0:24], high_x[24:48])
-        copies = [
-            pltpu.make_async_remote_copy(
-                src_ref=send_buf.at[s, way], dst_ref=recv_buf.at[s, way],
-                send_sem=step_send.at[s, way], recv_sem=step_recv.at[s, way],
-                device_id=other, device_id_type=MESH,
-            )
-            for way, other in enumerate((before_id, after_id))
-        ]
-        copies[1].start()
-        copies[0].start()
-        product = jnp.dot(oper_ref[2 * OUTER :, :], x, preferred_element_type=f32)
-        summed(product, INNER, 15 - SHARED, 96)
+        for copy in exchange(s)[::-1]:
+            copy.start()
+        force = known_s[OUTER : OUTER + INNER, :]
+        summed(force + changed(OUTER, INNER) if follow else force, 15 - SHARED, 96)
         low_sum = low_x + moved(split_two(high_x), to_low)
         high_sum = high_x + moved(split_two(low_x), to_high)
-        advance(96, 144, mass_of(16, 48), f_s[96:240, :])
-        copies[1].wait()
-        copies[0].wait()
-        low_sum = low_sum + moved(split_two(unpacked(recv_buf[s, 1])), from_before)
-        high_sum = high_sum + moved(split_two(unpacked(recv_buf[s, 0])), from_after)
-        advance(0, 48, mass_of(0, 16), low_sum)
-        advance(48, 48, mass_of(64, 16), high_sum)
+        advance(96, 144, thrice(m_s[16:64, :]), f_s[96:240, :])
+        advance(0, 48, thrice(m_s[0:16, :]), low_sum)
+        advance(48, 48, thrice(m_s[64:80, :]), high_sum)
+
+    def follow_on(s, carry):
+        substep(s, True)
+        know(s + 1)
         return carry
 
-    lax.fori_loop(0, substeps, substep, 0)
-
-    for ref in (u_s, v_s):
-        for c in range(3):
-            at = (0 if ref is u_s else 96) + c * 32
-            for a in range(2):
-                one, two = block_at(c, a), block_at(c, a + 2)
-                back_out[at + a * 16 : at + a * 16 + 16, :] = jnp.where(
-                    half16, ref[one : one + 16, :], ref[two : two + 16, :]
-                )
+    know(0)
+    substep(0, False)
+    know(1)
+    lax.fori_loop(1, substeps - 1, follow_on, 0)
+    substep(substeps - 1, True)
+
+    def back(part):
+        rows = slice(part * 96, part * 96 + 96)
+        return bulk(back_out.at[rows], back_in.at[rows], 2 + part, home_id)
+
+    for part, a in enumerate((1, 0)):
+        if part == 1:
+            arrived(substeps - 1)
+        for k in range(6):
+            ref, at = (u_s if k < 3 else v_s), part * 96 + k * 16
+            one, two = block_at(k % 3, a), block_at(k % 3, a + 2)
+            back_out[at : at + 16, :] = jnp.where(
+                half16, ref[one : one + 16, :], ref[two : two + 16, :]
+            )
+        if folded:
+
+            @pl.when(away)
+            def _():
+                back(part).start()
+
     if folded:
 
         @pl.when(away)
         def _():
-            back = bulk(back_out, back_in, 1, home_id)
-            back.start()
-            back.wait()
+            for part in range(2):
+                back(part).wait()
+            final_ref[...] = back_in[...]
 
         @pl.when(jnp.logical_not(away))
         def _():
-            back_in[...] = back_out[...]
-
-    final_ref[...] = (back_in if folded else back_out)[...]
+            final_ref[...] = back_out[...]
+    else:
+        final_ref[...] = back_out[...]
 
 
 def reorder(final_ref, place_ref, out_u_ref, out_v_ref):
@@ -488,9 +580,10 @@
 
     def scatter_step(t, kept):
         here = place_row == t
+        first = jnp.where(t < 16, t + 96, t - 16)
         new = []
         for k in range(6):
-            row = final_ref[pl.ds(k * 32 + t, 1), :]
+            row = final_ref[pl.ds(k * 16 + first, 1), :]
             got = jnp.take_along_axis(
                 jnp.broadcast_to(row, (32, 128)), place_lane, axis=1, mode="promise_in_bounds"
             )
@@ -532,10 +625,11 @@
             V((64, 4096), bf16), V((128, 4096), bf16),
             V((256, 128), f32), V((256, 128), f32), V((80, 128), f32), V((256, 128), f32),
             V((2 * TOTAL, 128), bf16), V((8, 128), f32),
+            V((OUTER + INNER, 128), f32), V((2 * DELTA, 128), bf16), V((DELTA, 128), f32),
             V((ROWS, 128), f32), V((ROWS, 128), f32), V((192, 128), f32), V((192, 128), f32),
             V((72, 128), f32), V((72, 128), f32), V((8, 128), f32), V((8, 128), f32),
             V((substeps, 2, 24, 128), f32), V((substeps, 2, 24, 128), f32),
-            S((2,)), S((2,)), S((substeps, 2)), S((substeps, 2)), S((2,)), S((2,)),
+            S((2,)), S((2,)), S((substeps, 2)), S((substeps, 2)), S((4,)), S((4,)),
         ],
         compiler_params=pltpu.CompilerParams(
             collective_id=0, has_side_effects=True, vmem_limit_bytes=63 * 1024 * 1024

time: 50.5 us -> 47.3 us (0.937)
  Pallas kernels: 49.6 us -> 46.5 us
    pallas_call x1, Pallas kernels: 45.4 us -> 42.2 us  [per_device(): pl.pallas_call(functools.partial(kernel, folded), out_shape=held, in_spec...]
where the time goes in v3:
time: 47.3 us; the launch traced here: 47.1 us
  Pallas kernels  46.5 us (98%)
  between operations  0.64 us (1%)
    pallas_call x1, Pallas kernels, per_device(): pl.pallas_call(functools.partial(kernel, folded), out_shape=held, in_spec...  42.2 us
    pallas_call x1, Pallas kernels, per_device(): pl.pallas_call(reorder, out_shape=(shape, shape), in_specs=[vmem] * 2, ou...  4.24 us

profile of v3, /device:TPU:0, one launch (start us, length us, event | category | flops | bytes accessed | tf_op | source)
XLA Modules:
  0.0 47.1 jit_solution(54966811228238531)
XLA Ops:
  0.6 42.2 %shard_map.104 = (f32[192,128]{1,0:T(8,128)}, s32[64,128]{1,0:T(8,128)}) custom-call(f32[3,4096]{1,0:T(4,128)} %disp_hbm.1, f32[3,4096]{1,0:T(4,128)} %vel_hbm.1, f32[32,128]{1,0:T(8,128)} %bitcast.7, s32[1,64]{1,0:T(1,128)} %bitcast.9, f32[1,64]{1,0:T(1,128)} %bitcast.10, f32[1,64]{1,0:T(1,128)} %bitcast.11, s32[64,125]{1,0:T(8,128)} %bitcast.6, ...), custom_call_target="tpu_custom_call" | custom-call | tf_op jit(solution)/shard_map/pallas_call | solution.py:618
  42.9 4.2 %shard_map.105 = (f32[3,4096]{1,0:T(4,128)}, f32[3,4096]{1,0:T(4,128)}) custom-call(f32[192,128]{1,0:T(8,128)} %get-tuple-element.4.final_ref, s32[64,128]{1,0:T(8,128)} %get-tuple-element.5.place_ref), custom_call_target="tpu_custom_call" | custom-call | tf_op jit(solution)/shard_map/pallas_call | solution.py:638

commit v4 on v3

--- a/solution.py
+++ b/solution.py
@@ -141,7 +141,7 @@
     folded, disp_hbm, vel_hbm, mass_hbm, level_hbm, lame_hbm, shear_hbm, conn_hbm, owner_hbm, oper_hbm,
     final_ref, place_ref,
     disp_ref, vel_ref, mass_ref, level_ref, lame_ref, shear_ref, conn_ref, owner_ref, oper_ref, load_sem,
-    conn_s, tile_s, pick_s, hot_hi, hot_lo, u_s, v_s, m_s, f_s, x_s, elem_s, known_s, change_s, rate_s,
+    conn_s, tile_s, pick_s, hot_hi, hot_lo, u_s, v_s, m_s, f_s, x_s, elem_s, known_s, change_s, rate_s, value_s, edge_s,
     pack_out, pack_in, back_out, back_in,
     low_out, low_in, name_out, name_in, send_buf, recv_buf,
     init_send, init_recv, step_send, step_recv, bulk_send, bulk_recv,
@@ -233,7 +233,7 @@
             return tuple(new)
 
         start = tuple(jnp.zeros((32, 128), f32) for _ in range(3 * len(refs) + len(singles)))
-        return list(lax.fori_loop(0, 32, gather_step, start, unroll=4))
+        return list(lax.fori_loop(0, 32, gather_step, start, unroll=32))
 
     for load in loads[1:8]:
         load.wait()
@@ -344,6 +344,7 @@
             ref[at : at + 16, :] = (low if a < 2 else high)[a % 2 * 16 : a % 2 * 16 + 16]
     u_s[MAIN : MAIN + 16, :] = jnp.zeros((16, 128), f32)
     f_s[MAIN : MAIN + 16, :] = jnp.zeros((16, 128), f32)
+    edge_s[...] = jnp.zeros((64, 128), f32)
     elem_s[...] = held[PARAMS_AT : PARAMS_AT + 8, :]
     slot_low = elem_s[0:1, :]
     name_row = [held[NAMES_AT + k : NAMES_AT + k + 1, :] for k in range(8)]
@@ -461,6 +462,11 @@
             for way, other in enumerate((before_id, after_id))
         ]
 
+    def worked(first, size, columns, x_ref):
+        rows = slice(2 * first, 2 * (first + size))
+        product = jnp.dot(oper_ref[rows, columns], x_ref[...], preferred_element_type=f32)
+        return product[0:size] + product[size:]
+
     def know(s):
         u = u_s[0:MAIN, :].reshape(15, 16, 128)
         faces = moved(split_three(u[:, 0:8].reshape(FACE, 128)), spread)
@@ -477,11 +483,8 @@
         values = jnp.concatenate(main + face + [edge, jnp.zeros((8, 128), f32)], axis=0)
         for k, weight in enumerate(weights(s)):
             x_s[k * TOTAL : (k + 1) * TOTAL, :] = split_two(values * weight)
-        x = x_s[...]
-        for first, size in ((0, OUTER), (OUTER, INNER)):
-            rows = slice(2 * first, 2 * (first + size))
-            product = jnp.dot(oper_ref[rows, 0 : 2 * TOTAL], x, preferred_element_type=f32)
-            known_s[first : first + size, :] = product[0:size] + product[size:]
+        value_s[...] = values
+        known_s[...] = worked(0, OUTER, slice(0, 2 * TOTAL), x_s)
 
     def arrived(s):
         for copy in exchange(s)[::-1]:
@@ -505,25 +508,31 @@
         )
         return jnp.concatenate([main, substep_length * rest * rate_s[96:192, :]], axis=0)
 
-    def changed(first, size):
-        rows = slice(2 * first, 2 * (first + size))
-        product = jnp.dot(oper_ref[rows, 2 * TOTAL :], change_s[...], preferred_element_type=f32)
-        return product[0:size] + product[size:]
-
     def substep(s, follow):
         if follow:
             change = arrived(s - 1)
             for k, weight in enumerate(weights(s)):
                 change_s[k * DELTA : (k + 1) * DELTA, :] = split_two(change * weight)
-        force = known_s[0:OUTER, :]
-        summed(force + changed(0, OUTER) if follow else force, SHARED, 0)
+        force = known_s[...]
+        if follow:
+            force = force + worked(0, OUTER, slice(2 * TOTAL, 2 * TOTAL + 2 * DELTA), change_s)
+        summed(force, SHARED, 0)
         low_x, high_x = f_s[0:48, :], f_s[48:96, :]
         send_buf[s, 0] = jnp.where(half24, low_x[0:24], low_x[24:48])
         send_buf[s, 1] = jnp.where(half24, high_x[0:24], high_x[24:48])
         for copy in exchange(s)[::-1]:
             copy.start()
-        force = known_s[OUTER : OUTER + INNER, :]
-        summed(force + changed(OUTER, INNER) if follow else force, 15 - SHARED, 96)
+        if follow:
+            edge_s[0:48, :] = change[144:192]
+            edge = jnp.where(row16[0:8] < SHARED, edge_s[pl.ds(0, 8, stride=8), :], 0.0)
+            none = jnp.zeros((8, 128), f32)
+            last = jnp.concatenate([none, edge, none, none], axis=0)
+            for at, part in ((0, change[0:96]), (MAIN, change[96:144]), (TOTAL - 32, last)):
+                size = part.shape[0]
+                full = value_s[at : at + size, :] + part
+                for k, weight in enumerate(weights(s)):
+                    x_s[k * TOTAL + at : k * TOTAL + at + size, :] = split_two(full * weight)
+        summed(worked(OUTER, INNER, slice(0, 2 * TOTAL), x_s), 15 - SHARED, 96)
         low_sum = low_x + moved(split_two(high_x), to_low)
         high_sum = high_x + moved(split_two(low_x), to_high)
         advance(96, 144, thrice(m_s[16:64, :]), f_s[96:240, :])
@@ -591,7 +600,7 @@
         return tuple(new)
 
     done = lax.fori_loop(
-        0, 32, scatter_step, tuple(jnp.zeros((32, 128), f32) for _ in range(6)), unroll=4
+        0, 32, scatter_step, tuple(jnp.zeros((32, 128), f32) for _ in range(6)), unroll=32
     )
     for k in range(6):
         ref = out_u_ref if k < 3 else out_v_ref
@@ -625,7 +634,8 @@
             V((64, 4096), bf16), V((128, 4096), bf16),
             V((256, 128), f32), V((256, 128), f32), V((80, 128), f32), V((256, 128), f32),
             V((2 * TOTAL, 128), bf16), V((8, 128), f32),
-            V((OUTER + INNER, 128), f32), V((2 * DELTA, 128), bf16), V((DELTA, 128), f32),
+            V((OUTER, 128), f32), V((2 * DELTA, 128), bf16), V((DELTA, 128), f32),
+            V((TOTAL, 128), f32), V((64, 128), f32),
             V((ROWS, 128), f32), V((ROWS, 128), f32), V((192, 128), f32), V((192, 128), f32),
             V((72, 128), f32), V((72, 128), f32), V((8, 128), f32), V((8, 128), f32),
             V((substeps, 2, 24, 128), f32), V((substeps, 2, 24, 128), f32),

time: 47.3 us -> 45.8 us (0.968)
  Pallas kernels: 46.5 us -> 44.9 us
    pallas_call x1, Pallas kernels: 42.2 us -> 41.2 us  [per_device(): pl.pallas_call(functools.partial(kernel, folded), out_shape=held, in_spec...]
where the time goes in v4:
time: 45.8 us; the launch traced here: 45.6 us
  Pallas kernels  44.9 us (98%)
  between operations  0.64 us (1%)
    pallas_call x1, Pallas kernels, per_device(): pl.pallas_call(functools.partial(kernel, folded), out_shape=held, in_spec...  41.2 us
    pallas_call x1, Pallas kernels, per_device(): pl.pallas_call(reorder, out_shape=(shape, shape), in_specs=[vmem] * 2, ou...  3.79 us

profile of v4, /device:TPU:0, one launch (start us, length us, event | category | flops | bytes accessed | tf_op | source)
XLA Modules:
  0.0 45.6 jit_solution(13920818510079359511)
XLA Ops:
  0.6 41.2 %shard_map.104 = (f32[192,128]{1,0:T(8,128)}, s32[64,128]{1,0:T(8,128)}) custom-call(f32[3,4096]{1,0:T(4,128)} %disp_hbm.1, f32[3,4096]{1,0:T(4,128)} %vel_hbm.1, f32[32,128]{1,0:T(8,128)} %bitcast.7, s32[1,64]{1,0:T(1,128)} %bitcast.9, f32[1,64]{1,0:T(1,128)} %bitcast.10, f32[1,64]{1,0:T(1,128)} %bitcast.11, s32[64,125]{1,0:T(8,128)} %bitcast.6, ...), custom_call_target="tpu_custom_call" | custom-call | tf_op jit(solution)/shard_map/pallas_call | solution.py:627
  41.8 3.8 %shard_map.105 = (f32[3,4096]{1,0:T(4,128)}, f32[3,4096]{1,0:T(4,128)}) custom-call(f32[192,128]{1,0:T(8,128)} %get-tuple-element.4.final_ref, s32[64,128]{1,0:T(8,128)} %get-tuple-element.5.place_ref), custom_call_target="tpu_custom_call" | custom-call | tf_op jit(solution)/shard_map/pallas_call | solution.py:648

commit v5 on v4

--- a/solution.py
+++ b/solution.py
@@ -22,7 +22,7 @@
 HIGH = [(4, 0), (4, 1), (4, 2), (4, 3), (1, 4), (2, 4), (3, 4), (0, 4)]
 PLANES = [(c, a) for a in (0, 4) for c in range(3)] + [(c, a) for c in range(3) for a in (1, 2, 3)]
 MAIN, FACE, TOTAL = 240, 120, 384
-SHARED, OUTER, INNER, DELTA = 6, 160, 240, 192
+SHARED, OUTER, INNER, DELTA = 6, 192, 288, 192
 
 
 def lobatto_tables():
@@ -66,15 +66,18 @@
 
     taken = ordered(PLANES)
     shared = ordered(PLANES[:SHARED])
-    spots = np.concatenate([np.arange(SHARED * 24), SHARED * 24 + 8 * np.arange(SHARED)])
+    def spots(count):
+        return np.concatenate([np.arange(count * 24), count * 24 + 8 * np.arange(count)])
+
     parts = []
     for planes, size in ((PLANES[:SHARED], OUTER), (PLANES[SHARED:], INNER)):
         given = ordered(planes)
+        into = spots(len(planes))
         part = np.zeros((size, 2 * TOTAL + 2 * DELTA))
         for k, table in enumerate((lame.reshape(375, 375), shear.reshape(375, 375))):
-            part[: len(given), k * TOTAL : k * TOTAL + len(taken)] = table[np.ix_(given, taken)]
+            part[np.ix_(into, k * TOTAL + np.arange(len(taken)))] = table[np.ix_(given, taken)]
             at = 2 * TOTAL + k * DELTA
-            part[: len(given), at + spots] = table[np.ix_(given, shared)]
+            part[np.ix_(into, at + spots(SHARED))] = table[np.ix_(given, shared)]
         high = part.astype(jnp.bfloat16)
         parts += [high, (part - high.astype(np.float64)).astype(jnp.bfloat16)]
     return np.concatenate(parts, axis=0)
@@ -141,7 +144,7 @@
     folded, disp_hbm, vel_hbm, mass_hbm, level_hbm, lame_hbm, shear_hbm, conn_hbm, owner_hbm, oper_hbm,
     final_ref, place_ref,
     disp_ref, vel_ref, mass_ref, level_ref, lame_ref, shear_ref, conn_ref, owner_ref, oper_ref, load_sem,
-    conn_s, tile_s, pick_s, hot_hi, hot_lo, u_s, v_s, m_s, f_s, x_s, elem_s, known_s, change_s, rate_s, value_s, edge_s,
+    conn_s, tile_s, pick_s, hot_hi, hot_lo, u_s, v_s, m_s, x_s, elem_s, known_s, change_s, rate_s, value_s, edge_s,
     pack_out, pack_in, back_out, back_in,
     low_out, low_in, name_out, name_in, send_buf, recv_buf,
     init_send, init_recv, step_send, step_recv, bulk_send, bulk_recv,
@@ -343,7 +346,6 @@
             at = block_at(k % 3, a) if k < 6 else a * 16
             ref[at : at + 16, :] = (low if a < 2 else high)[a % 2 * 16 : a % 2 * 16 + 16]
     u_s[MAIN : MAIN + 16, :] = jnp.zeros((16, 128), f32)
-    f_s[MAIN : MAIN + 16, :] = jnp.zeros((16, 128), f32)
     edge_s[...] = jnp.zeros((64, 128), f32)
     elem_s[...] = held[PARAMS_AT : PARAMS_AT + 8, :]
     slot_low = elem_s[0:1, :]
@@ -359,9 +361,10 @@
     spread = jnp.concatenate([spread, spread], axis=0)
     spread_edge = jnp.concatenate([to_edge, to_edge], axis=0)
     collect = jnp.concatenate(
-        [same(name_col[1], name_row[0]), same(name_col[3], name_row[2])], axis=1
-    )
-    collect_edge = same(name_col[5], name_row[4])
+        [same(name_col[1], name_row[0]), same(name_col[3], name_row[2]), same(name_col[5], name_row[4])],
+        axis=1,
+    )
+    collect = jnp.concatenate([collect, collect], axis=0)
     to_high = same(name_col[6], name_row[7])
     to_low = same(name_col[7], name_row[6])
 
@@ -425,21 +428,21 @@
         v_s[rows, :] = speed
         u_s[rows, :] = u_s[rows, :] + substep_length * speed
 
-    def summed(force, planes, first):
-        force = force + pltpu.roll(force, 64, axis=1)
+    def summed(force, planes):
         main, faces = planes * 16, planes * 24
-        moved_face = moved(split_two(force[main:faces]), collect)
-        along_y = moved_face[:, 0:128].reshape(planes, 8, 128)
-        along_z = moved_face[:, 128:256].reshape(planes, 8, 128)
+        high = force[main:].astype(bf16)
+        rest = (force[main:] - high.astype(f32)).astype(bf16)
+        given = moved(jnp.concatenate([high, rest], axis=1), collect)
+        along_y = given[0 : faces - main, 0:128].reshape(planes, 8, 128)
+        along_z = given[0 : faces - main, 128:256].reshape(planes, 8, 128)
+        edge = given[faces - main :, 256:384].reshape(planes, 8, 128)
         row = row8[0:planes]
-        low = jnp.where(row < 4, along_y, jnp.where(row < 7, along_z, 0.0))
+        low = edge + jnp.where(row < 4, along_y, jnp.where(row < 7, along_z, 0.0))
         low = low + jnp.where(row == 0, pltpu.roll(along_z, 1, axis=1), 0.0)
-        both = force[0:main].reshape(planes, 2, 8, 128)
+        both = force[0:main] + pltpu.roll(force[0:main], 64, axis=1)
+        both = both.reshape(planes, 2, 8, 128)
         both = jnp.concatenate([both[:, 0:1] + low[:, None], both[:, 1:2]], axis=1)
-        f_s[first : first + main, :] = both.reshape(main, 128)
-        edge = moved(split_two(force[faces:]), collect_edge)[0:planes]
-        at = pl.ds(first, planes, stride=16)
-        f_s[at, :] = f_s[at, :] + edge
+        return both.reshape(main, 128)
 
     def unpacked(packed):
         turned = pltpu.roll(packed, 64, axis=1)
@@ -516,8 +519,8 @@
         force = known_s[...]
         if follow:
             force = force + worked(0, OUTER, slice(2 * TOTAL, 2 * TOTAL + 2 * DELTA), change_s)
-        summed(force, SHARED, 0)
-        low_x, high_x = f_s[0:48, :], f_s[48:96, :]
+        force = summed(force, SHARED)
+        low_x, high_x = force[0:48], force[48:96]
         send_buf[s, 0] = jnp.where(half24, low_x[0:24], low_x[24:48])
         send_buf[s, 1] = jnp.where(half24, high_x[0:24], high_x[24:48])
         for copy in exchange(s)[::-1]:
@@ -532,10 +535,10 @@
                 full = value_s[at : at + size, :] + part
                 for k, weight in enumerate(weights(s)):
                     x_s[k * TOTAL + at : k * TOTAL + at + size, :] = split_two(full * weight)
-        summed(worked(OUTER, INNER, slice(0, 2 * TOTAL), x_s), 15 - SHARED, 96)
+        inner = summed(worked(OUTER, INNER, slice(0, 2 * TOTAL), x_s), 15 - SHARED)
         low_sum = low_x + moved(split_two(high_x), to_low)
         high_sum = high_x + moved(split_two(low_x), to_high)
-        advance(96, 144, thrice(m_s[16:64, :]), f_s[96:240, :])
+        advance(96, 144, thrice(m_s[16:64, :]), inner)
         advance(0, 48, thrice(m_s[0:16, :]), low_sum)
         advance(48, 48, thrice(m_s[64:80, :]), high_sum)
 
@@ -632,7 +635,7 @@
         scratch_shapes=[V(x.shape, x.dtype) for x in operands] + [S((9,))] + [
             V((128, 128), f32), V((128, 128), f32), V((32, 128), jnp.int32),
             V((64, 4096), bf16), V((128, 4096), bf16),
-            V((256, 128), f32), V((256, 128), f32), V((80, 128), f32), V((256, 128), f32),
+            V((256, 128), f32), V((256, 128), f32), V((80, 128), f32),
             V((2 * TOTAL, 128), bf16), V((8, 128), f32),
             V((OUTER, 128), f32), V((2 * DELTA, 128), bf16), V((DELTA, 128), f32),
             V((TOTAL, 128), f32), V((64, 128), f32),

time: 45.8 us -> 45.4 us (level)
  no operation moved by 1% of the time
where the time goes in v5:
time: 45.4 us; the launch traced here: 45.2 us
  Pallas kernels  44.6 us (98%)
  between operations  0.64 us (1%)
    pallas_call x1, Pallas kernels, per_device(): pl.pallas_call(functools.partial(kernel, folded), out_shape=held, in_spec...  40.8 us
    pallas_call x1, Pallas kernels, per_device(): pl.pallas_call(reorder, out_shape=(shape, shape), in_specs=[vmem] * 2, ou...  3.79 us

profile of v5, /device:TPU:0, one launch (start us, length us, event | category | flops | bytes accessed | tf_op | source)
XLA Modules:
  0.0 45.2 jit_solution(12638723430398262358)
XLA Ops:
  0.6 40.8 %shard_map.104 = (f32[192,128]{1,0:T(8,128)}, s32[64,128]{1,0:T(8,128)}) custom-call(f32[3,4096]{1,0:T(4,128)} %disp_hbm.1, f32[3,4096]{1,0:T(4,128)} %vel_hbm.1, f32[32,128]{1,0:T(8,128)} %bitcast.7, s32[1,64]{1,0:T(1,128)} %bitcast.9, f32[1,64]{1,0:T(1,128)} %bitcast.10, f32[1,64]{1,0:T(1,128)} %bitcast.11, s32[64,125]{1,0:T(8,128)} %bitcast.6, ...), custom_call_target="tpu_custom_call" | custom-call | tf_op jit(solution)/shard_map/pallas_call | solution.py:630
  41.4 3.8 %shard_map.105 = (f32[3,4096]{1,0:T(4,128)}, f32[3,4096]{1,0:T(4,128)}) custom-call(f32[192,128]{1,0:T(8,128)} %get-tuple-element.4.final_ref, s32[64,128]{1,0:T(8,128)} %get-tuple-element.5.place_ref), custom_call_target="tpu_custom_call" | custom-call | tf_op jit(solution)/shard_map/pallas_call | solution.py:651

commit v6 on v5

--- a/solution.py
+++ b/solution.py
@@ -550,7 +550,7 @@
     know(0)
     substep(0, False)
     know(1)
-    lax.fori_loop(1, substeps - 1, follow_on, 0)
+    lax.fori_loop(1, substeps - 1, follow_on, 0, unroll=2)
     substep(substeps - 1, True)
 
     def back(part):

time: 45.4 us -> 45.4 us (level)
  no operation moved by 1% of the time
where the time goes in v6:
time: 45.4 us; the launch traced here: 45.2 us
  Pallas kernels  44.6 us (98%)
  between operations  0.64 us (1%)
    pallas_call x1, Pallas kernels, per_device(): pl.pallas_call(functools.partial(kernel, folded), out_shape=held, in_spec...  40.8 us
    pallas_call x1, Pallas kernels, per_device(): pl.pallas_call(reorder, out_shape=(shape, shape), in_specs=[vmem] * 2, ou...  3.79 us

profile of v6, /device:TPU:0, one launch (start us, length us, event | category | flops | bytes accessed | tf_op | source)
XLA Modules:
  0.0 45.2 jit_solution(17923154021589484922)
XLA Ops:
  0.6 40.8 %shard_map.104 = (f32[192,128]{1,0:T(8,128)}, s32[64,128]{1,0:T(8,128)}) custom-call(f32[3,4096]{1,0:T(4,128)} %disp_hbm.1, f32[3,4096]{1,0:T(4,128)} %vel_hbm.1, f32[32,128]{1,0:T(8,128)} %bitcast.7, s32[1,64]{1,0:T(1,128)} %bitcast.9, f32[1,64]{1,0:T(1,128)} %bitcast.10, f32[1,64]{1,0:T(1,128)} %bitcast.11, s32[64,125]{1,0:T(8,128)} %bitcast.6, ...), custom_call_target="tpu_custom_call" | custom-call | tf_op jit(solution)/shard_map/pallas_call | solution.py:630
  41.4 3.8 %shard_map.105 = (f32[3,4096]{1,0:T(4,128)}, f32[3,4096]{1,0:T(4,128)}) custom-call(f32[192,128]{1,0:T(8,128)} %get-tuple-element.4.final_ref, s32[64,128]{1,0:T(8,128)} %get-tuple-element.5.place_ref), custom_call_target="tpu_custom_call" | custom-call | tf_op jit(solution)/shard_map/pallas_call | solution.py:651
